TPU v7x, 512 devices: a whole 4x8x8 slice. The times are simulated.
512 devices in a mesh: row: 32 (over x, z_hi, core), col: 16 (over y, z_lo).
Axes of the slice: x: 4, y: 8, z: 8 (z_hi: 4, z_lo: 2; z = z_hi * 2 + z_lo), core: 2. Of those that a mesh axis runs over, the one named last changes fastest.
Arguments:
- layer_input: bfloat16 [1024, 6144], P('row', 'col'), may hold values from -6 to 6
- output_grad: bfloat16 [1024, 6144], P('row', 'col'), may hold values from -1.5 to 1.5
- preact: bfloat16 [1024, 24576], P('col', 'row'), may hold values from -8 to 8
- weight_in: bfloat16 [6144, 24576], P('col', 'row'), may hold values from -0.078125 to 0.078125
- weight_out: bfloat16 [24576, 6144], P('row', 'col'), may hold values from -0.0390625 to 0.0390625
Outputs:
- input_grad: bfloat16 [1024, 6144], P('row', 'col')
- grad_in: float32 [6144, 24576], P('col', 'row')
- grad_out: float32 [24576, 6144], P('row', 'col')
All inputs are finite; a program needn't handle non-finite values.
Results may differ from a plain program's by a relative error of at most 0.0049.
Values may be sent and summed in bfloat16 or wider, within the bound.
A program may use at most 64 MiB of HBM per device.

v0:
```python
import math

import jax
import jax.numpy as jnp
from jax import lax
from jax.sharding import PartitionSpec as P


def gelu_parts(pre):
    cdf = 0.5 * (1.0 + jax.scipy.special.erf(pre / math.sqrt(2.0)))
    pdf = jnp.exp(-0.5 * pre * pre) / math.sqrt(2.0 * math.pi)
    return (pre * cdf, cdf + pre * pdf)


def last_dims(left, right):
    return lax.dot_general(
        left, right, (((1,), (1,)), ((), ())), preferred_element_type=jnp.float32
    )


def first_dims(left, right):
    return lax.dot_general(
        left, right, (((0,), (0,)), ((), ())), preferred_element_type=jnp.float32
    )


def hidden_local(preact, act_grad):
    value, slope = gelu_parts(preact.astype(jnp.float32))
    return (value.astype(jnp.bfloat16), (act_grad * slope).astype(jnp.bfloat16))


def on_device(layer_input, output_grad, preact, weight_in, weight_out):
    inputs_all, grads_all = (
        lax.all_gather(layer_input, "row", axis=0, tiled=True),
        lax.all_gather(output_grad, "row", axis=0, tiled=True),
    )
    rows = grads_all
    act_grad = lax.psum_scatter(last_dims(rows, weight_out), "col", scatter_dimension=0, tiled=True)
    activ, hid_grad = hidden_local(preact, act_grad)
    activ_all, hid_all = (
        lax.all_gather(activ, "col", axis=0, tiled=True),
        lax.all_gather(hid_grad, "col", axis=0, tiled=True),
    )
    grad_out = first_dims(activ_all, grads_all)
    rows = hid_all
    input_grad = lax.psum_scatter(
        last_dims(rows, weight_in), "row", scatter_dimension=0, tiled=True
    ).astype(jnp.bfloat16)
    grad_in = first_dims(inputs_all, hid_all)
    return (input_grad, grad_in, grad_out)


def solution(mesh):
    in_specs = (P("row", "col"), P("row", "col"), P("col", "row"), P("col", "row"), P("row", "col"))
    out_specs = (P("row", "col"), P("col", "row"), P("row", "col"))
    return jax.shard_map(
        on_device, mesh=mesh, in_specs=in_specs, out_specs=out_specs, check_vma=False
    )
```

profile of v0, /device:TPU:1, one launch (start us, length us, event | category | flops | bytes accessed | tf_op | source)
XLA Modules:
  0.0 403.4 jit_solution(1138744188084297203)
XLA Ops:
  7.2 0.0 copy-start
  7.2 0.0 reduce-scatter.3.cloned.1.call-start
  7.2 54.1 %all_gather.12 = bf16[1024,384]{1,0:T(8,128)(2,1)S(1)} all-gather(bf16[32,384]{1,0:T(8,128)(2,1)} %param.6), channel_id=1, replica_groups=mesh['row'=32,'col'=16] {'row'}, dimensions={0}, use_global_device_ids=true | all-gather | bytes 811008 | tf_op jit(solution)/shard_map/all_gather | solution.py:35
  61.4 0.0 copy-done
  61.4 2.6 fusion.9
  64.0 0.0 copy-start.3
  64.0 0.0 copy-start.2
  64.0 0.0 reduce-scatter.3.cloned.1.call-update
  64.0 0.0 all-gather.3.cloned.1.call-start
  64.1 74.9 %reduce-scatter.3.cloned.1.call-done = f32[64,768]{1,0:T(8,128)} async-done(((f32[1024,768]{1,0:T(8,128)}), f32[64,768]{1,0:T(8,128)}) %reduce-scatter.3.cloned.1.call-update) | async-done | bytes 196624 | tf_op jit(solution)/shard_map/reduce_scatter | solution.py:38
  139.0 0.0 copy-done.3
  139.0 1.7 fusion.8
  140.7 0.0 all-gather.3.cloned.1.call-update
  140.7 0.0 all-gather.5.cloned.1.call-start
  140.8 0.7 all-gather.5.cloned.1.call-update
  141.5 0.0 reduce-scatter.5.cloned.1.call-start
  141.5 66.5 %all-gather.3.cloned.1.call-done = bf16[1024,768]{1,0:T(8,128)(2,1)} async-done(((bf16[64,768]{1,0:T(8,128)(2,1)}), bf16[1024,768]{1,0:T(8,128)(2,1)}) %all-gather.3.cloned.1.call-update) | async-done | bytes 1572880 | tf_op jit(solution)/shard_map/all_gather | solution.py:42
  208.0 0.0 copy-done.2
  208.0 3.6 fusion.10
  211.5 0.0 copy-start.1
  211.5 0.0 reduce-scatter.5.cloned.1.call-update
  211.6 58.6 %all_gather.14 = bf16[1024,384]{1,0:T(8,128)(2,1)S(1)} all-gather(bf16[32,384]{1,0:T(8,128)(2,1)} %param.5), channel_id=1, replica_groups=mesh['row'=32,'col'=16] {'row'}, dimensions={0}, use_global_device_ids=true | all-gather | bytes 811008 | tf_op jit(solution)/shard_map/all_gather | solution.py:34
  270.2 0.0 copy-done.1
  270.2 2.0 convolution_bitcast_fusion
  272.2 2.7 copy.8
  274.9 10.5 %all-gather.5.cloned.1.call-done = bf16[1024,768]{1,0:T(8,128)(2,1)} async-done(((bf16[64,768]{1,0:T(8,128)(2,1)}), bf16[1024,768]{1,0:T(8,128)(2,1)}) %all-gather.5.cloned.1.call-update) | async-done | bytes 1572880 | tf_op jit(solution)/shard_map/all_gather | solution.py:41
  285.3 3.4 fusion.11
  288.8 106.7 %reduce-scatter.5.cloned.1.call-done = f32[32,384]{1,0:T(8,128)} async-done(((f32[1024,384]{1,0:T(8,128)}), f32[32,384]{1,0:T(8,128)}) %reduce-scatter.5.cloned.1.call-update) | async-done | bytes 49168 | tf_op jit(solution)/shard_map/reduce_scatter | solution.py:46
  395.5 1.4 convert_element_type.14
Async XLA Ops:
  7.2 54.2 %copy-start = (bf16[768,384]{1,0:T(8,128)(2,1)S(1)}, bf16[768,384]{1,0:T(8,128)(2,1)}, u32[]{:S(2)}) copy-start(bf16[768,384]{1,0:T(8,128)(2,1)} %param.9) | copy-start | bytes 1769476
  7.2 131.8 %reduce-scatter.3.cloned.1.call-start = ((), (), s32[]{:S(2)}) async-start(), calls=%async_computation.2 | async-start | bytes 3342336 | tf_op jit(solution)/shard_map/reduce_scatter | solution.py:38
  64.0 75.0 %copy-start.3 = (bf16[64,768]{1,0:T(8,128)(2,1)S(1)}, bf16[64,768]{1,0:T(8,128)(2,1)}, u32[]{:S(2)}) copy-start(bf16[64,768]{1,0:T(8,128)(2,1)} %param.7) | copy-start | bytes 294916
  64.0 144.0 %copy-start.2 = (bf16[384,768]{1,0:T(8,128)(2,1)S(1)}, bf16[384,768]{1,0:T(8,128)(2,1)}, u32[]{:S(2)}) copy-start(bf16[384,768]{1,0:T(8,128)(2,1)} %param.8) | copy-start | bytes 1769476
  64.0 144.0 %all-gather.3.cloned.1.call-start = ((), (), s32[]{:S(2)}) async-start(), calls=%async_computation.3 | async-start | bytes 1671168 | tf_op jit(solution)/shard_map/all_gather | solution.py:42
  140.7 144.6 %all-gather.5.cloned.1.call-start = ((), (), s32[]{:S(2)}) async-start(), calls=%async_computation.5 | async-start | bytes 1671168 | tf_op jit(solution)/shard_map/all_gather | solution.py:41
  141.5 254.0 %reduce-scatter.5.cloned.1.call-start = ((), (), s32[]{:S(2)}) async-start(), calls=%async_computation.4 | async-start | bytes 1622016 | tf_op jit(solution)/shard_map/reduce_scatter | solution.py:46
  211.5 58.6 %copy-start.1 = (bf16[1024,768]{1,0:T(8,128)(2,1)S(1)}, bf16[1024,768]{1,0:T(8,128)(2,1)}, u32[]{:S(2)}) copy-start(bf16[1024,768]{1,0:T(8,128)(2,1)} %all-gather.3.cloned.1.call-done) | copy-start | bytes 4718596
Sparse Core Ops, SparseCore 0:
  64.1 74.8 reduce-scatter.2
  141.7 66.2 all-gather.2
  210.1 75.2 all-gather.4
  289.6 105.8 reduce-scatter.4
where the time goes:
time: 405 us; the launch traced here: 403 us
  waiting for transfers between devices  259 us (64%)
  blocking collectives  113 us (28%)
  between operations  13.8 us (3%)
  matrix products  11.6 us (3%)
    reduce_scatter x1, waiting for transfers between devices, on_device(): lax.psum_scatter(last_dims(rows, weight_in), 'row', scatter_dimension=0,...  107 us
    reduce_scatter x1, waiting for transfers between devices, on_device(): lax.psum_scatter(last_dims(rows, weight_out), 'col', scatter_dimension=0,...  74.9 us
    all_gather x1, waiting for transfers between devices, on_device(): lax.all_gather(hid_grad, 'col', axis=0, tiled=True)  66.5 us
    all_gather x1, blocking collectives, on_device(): lax.all_gather(layer_input, 'row', axis=0, tiled=True)  58.6 us
    all_gather x1, blocking collectives, on_device(): lax.all_gather(output_grad, 'row', axis=0, tiled=True)  54.1 us
    all_gather x1, waiting for transfers between devices, on_device(): lax.all_gather(activ, 'col', axis=0, tiled=True)  10.5 us
  transfers between devices with their start and end apart: 4, of which 4 were waited for; matrix products, arithmetic and copies ran while one was open for 3% of the time, Pallas kernels for 0%

commit v1 on v0

v1 whole, which is shorter than its diff:
```python
import math

import jax
import jax.numpy as jnp
from jax import lax
from jax.experimental import pallas as pl
from jax.experimental.pallas import tpu as pltpu
from jax.sharding import PartitionSpec as P

MESH = pl.DeviceIdType.MESH
BF, F32 = jnp.bfloat16, jnp.float32
TOK, DB, FB = 1024, 384, 768
T = 32
DELTAS = [(dx, dz) for dx in (2, 1, 3, 0) for dz in (2, 1, 3, 0) if (dx, dz) != (0, 0)]


def gelu_parts(pre):
    cdf = 0.5 * (1.0 + lax.erf(pre * (1.0 / math.sqrt(2.0))))
    pdf = jnp.exp(-0.5 * pre * pre) * (1.0 / math.sqrt(2.0 * math.pi))
    return pre * cdf, cdf + pre * pdf


def dot(a, b, ca, cb):
    return lax.dot_general(a, b, (((ca,), (cb,)), ((), ())), preferred_element_type=F32)


def kernel(
    li, og, pre, w_in_hbm, w_out_hbm, ig_out, gi_out, go_out,
    w_in, w_out, li_all, og_all, act_all, hid_all, li_t, slope, c_own, cz_send, cz_recv, r_send, r_recv,
    q_sib, q_in, q_own, q_send, q_recv, gi_v, go_v,
    og_ss, og_rs, ogs_ss, ogs_rs, li_ss, li_rs, lis_ss, lis_rs, ar_ss, ar_rs, az_ss, az_rs, hr_ss, hr_rs, hz_ss, hz_rs,
    cz_ss, cz_rs, rr_ss, rr_rs, qs_ss, qs_rs, q_ss, q_rs, loc,
):
    row, col = lax.axis_index("row"), lax.axis_index("col")
    x, zh, k = row // 8, (row // 2) % 4, row % 2
    y, zl = col // 2, col % 2

    def dev(x=x, zh=zh, k=k, y=y, zl=zl):
        return (x * 8 + zh * 2 + k, y * 2 + zl)

    sib, zpart = dev(k=1 - k), dev(zl=1 - zl)
    ynext = [dev(y=(y + 1) % 8), dev(y=(y + 7) % 8)]

    def peer(dx, dz):
        return (x + dx) % 4, (zh + dz) % 4

    def place(px, pz):
        return pz % 2, px * 2 + pz // 2

    mine = place(x, zh)
    started = []

    def send(src, dst, ss, rs, to):
        c = pltpu.make_async_remote_copy(src_ref=src, dst_ref=dst, send_sem=ss, recv_sem=rs, device_id=to, device_id_type=MESH)
        c.start()
        started.append(c)

    def arrive(dst, ss, rs):
        pltpu.make_async_remote_copy(src_ref=dst, dst_ref=dst, send_sem=ss, recv_sem=rs, device_id=sib, device_id_type=MESH).wait_recv()

    load_out = pltpu.make_async_copy(w_out_hbm, w_out, loc.at[0])
    load_in = pltpu.make_async_copy(w_in_hbm, w_in, loc.at[1])
    load_out.start()
    load_in.start()

    barrier = pltpu.get_barrier_semaphore()
    partners = [dev(x=px, zh=pz) for px, pz in (peer(*d) for d in DELTAS)] + [sib, zpart] + ynext
    for p in partners:
        pl.semaphore_signal(barrier, inc=1, device_id=p, device_id_type=MESH)

    og_all[k, mine[0], mine[1]] = og[...]
    li_all[k, mine[0], mine[1]] = li[...]
    for h in range(2):
        value, sl = gelu_parts(pre[pl.ds(h * T, T), :].astype(F32))
        act_all[h, zl, y] = value.astype(BF)
        slope[h] = sl
    pl.semaphore_wait(barrier, len(partners))

    def gather_send(own, full, ss, rs):
        for j, d in enumerate(DELTAS):
            px, pz = peer(*d)
            send(own, full.at[k, mine[0], mine[1]], ss.at[j], rs.at[j], dev(x=px, zh=pz))

    def gather_arrive(full, ss, rs, sss, srs):
        for j, d in enumerate(DELTAS):
            p = place(*peer(-d[0] + 4, -d[1] + 4))
            arrive(full.at[k, p[0], p[1]], ss.at[j], rs.at[j])
        send(full.at[k], full.at[k], sss, srs, sib)

    def gather_done(full, sss, srs):
        arrive(full.at[1 - k], sss, srs)

    def ring_step(full, s, rss, rrs, z=None):
        for h in range(2):
            for d in range(2):
                sg = 1 - 2 * d
                came = (y - sg * s + 8) % 8
                if s == 0:
                    ref = full.at[h, zl, y]
                elif s <= 3 or h == d:
                    ref = full.at[h, zl, came]
                    arrive(ref, rss.at[d, s - 1, h], rrs.at[d, s - 1, h])
                else:
                    continue
                if s <= 2 or (s == 3 and h == d):
                    send(ref, ref, rss.at[d, s, h], rrs.at[d, s, h], ynext[d])
                if z is not None:
                    pass_on(full, s, d, h, *z)

    def slot(s, d):
        return 0 if s == 0 else 7 if s == 4 else s + 3 * d

    def pass_on(full, s, d, h, zss, zrs):
        if (s == 0 and d == 1) or (s == 4 and h != d):
            return
        ref = full.at[h, zl, (y - (1 - 2 * d) * s + 8) % 8]
        send(ref, ref, zss.at[slot(s, d), h], zrs.at[slot(s, d), h], zpart)

    def passed(full, zss, zrs):
        for s in range(5):
            for d in range(2):
                for h in range(2):
                    if (s == 0 and d == 1) or (s == 4 and h != d):
                        continue
                    ref = full.at[h, 1 - zl, (y - (1 - 2 * d) * s + 8) % 8]
                    arrive(ref, zss.at[slot(s, d), h], zrs.at[slot(s, d), h])

    act_z, hid_z = (az_ss, az_rs), (hz_ss, hz_rs)
    gather_send(og, og_all, og_ss, og_rs)
    ring_step(act_all, 0, ar_ss, ar_rs, act_z)
    gather_arrive(og_all, og_ss, og_rs, ogs_ss, ogs_rs)
    ring_step(act_all, 1, ar_ss, ar_rs, act_z)

    load_out.wait()

    def partial(h, half, store):
        rows = og_all[h, half].reshape(8 * T, DB)

        def tile(n, _):
            cols = pl.ds(pl.multiple_of(n * 256, 256), 256)
            store(cols, dot(rows, w_out[cols, :], 1, 1).reshape(8, T, 256))
            return _

        lax.fori_loop(0, 3, tile, 0)

    def to_partner(h):
        def store(cols, v):
            cz_send[h, :, :, cols] = v.astype(BF)

        partial(h, 1 - zl, store)
        for d in (4, 3, 5, 2, 6, 1, 7, 0):
            at = (y + d) % 8
            send(cz_send.at[h, at], cz_recv.at[h, at], cz_ss.at[d, h], cz_rs.at[d, h], zpart)

    def to_self(h):
        def store(cols, v):
            c_own[h, :, :, cols] = v

        partial(h, zl, store)

    to_partner(k)
    gather_done(og_all, ogs_ss, ogs_rs)
    to_partner(1 - k)
    to_self(k)
    to_self(1 - k)
    ring_step(act_all, 2, ar_ss, ar_rs)

    def term(d, h):
        at = (y + d) % 8
        arrive(cz_recv.at[h, at], cz_ss.at[d, h], cz_rs.at[d, h])
        return c_own[h, at] + cz_recv[h, at].astype(F32)

    for s in range(4):
        for d in range(2):
            sg = 1 - 2 * d
            for h in (d, 1 - d):
                if s == 0 and h != d:
                    continue
                total = term((sg * (4 - s)) % 8, h)
                if s >= 2 or (s == 1 and h == d):
                    arrive(r_recv.at[d, s - 1, h], rr_ss.at[d, s - 1, h], rr_rs.at[d, s - 1, h])
                    total = total + r_recv[d, s - 1, h].astype(F32)
                r_send[d, s, h] = total.astype(BF)
                send(r_send.at[d, s, h], r_recv.at[d, s, h], rr_ss.at[d, s, h], rr_rs.at[d, s, h], ynext[d])
        if s == 0:
            gather_send(li, li_all, li_ss, li_rs)
        if s == 1:
            ring_step(act_all, 3, ar_ss, ar_rs)
        if s == 2:
            ring_step(act_all, 4, ar_ss, ar_rs)
            for t in (2, 3, 4):
                for d in range(2):
                    for h in range(2):
                        pass_on(act_all, t, d, h, *act_z)
    for h in range(2):
        total = term(0, h)
        for d in range(2):
            arrive(r_recv.at[d, 3, h], rr_ss.at[d, 3, h], rr_rs.at[d, 3, h])
            total = total + r_recv[d, 3, h].astype(F32)
        hid_all[h, zl, y] = (total * slope[h]).astype(BF)

    ring_step(hid_all, 0, hr_ss, hr_rs, hid_z)
    gather_arrive(li_all, li_ss, li_rs, lis_ss, lis_rs)
    passed(act_all, az_ss, az_rs)
    ring_step(hid_all, 1, hr_ss, hr_rs, hid_z)

    def go_tile(n, _):
        cols = pl.ds(pl.multiple_of(n * 256, 256), 256)
        go_v[cols, :] = dot(act_all[:, :, :, :, cols].reshape(TOK, 256), og_all[...].reshape(TOK, DB), 0, 0)
        return _

    lax.fori_loop(0, 3, go_tile, 0)
    store_go = pltpu.make_async_copy(go_v, go_out, loc.at[2])
    store_go.start()
    ring_step(hid_all, 2, hr_ss, hr_rs, hid_z)
    gather_done(li_all, lis_ss, lis_rs)
    li_t[...] = li_all[...].reshape(TOK, DB).T
    load_in.wait()
    ring_step(hid_all, 3, hr_ss, hr_rs, hid_z)
    ring_step(hid_all, 4, hr_ss, hr_rs, hid_z)

    def q_part(h, half):
        return dot(hid_all[h, half].reshape(8 * T, FB), w_in[...], 1, 1).reshape(8, T, DB)

    q_sib[zl] = q_part(1 - k, zl)
    send(q_sib.at[zl], q_in.at[zl], qs_ss.at[0], qs_rs.at[0], sib)
    q_own[zl] = q_part(k, zl)
    passed(hid_all, hz_ss, hz_rs)
    q_sib[1 - zl] = q_part(1 - k, 1 - zl)
    send(q_sib.at[1 - zl], q_in.at[1 - zl], qs_ss.at[1], qs_rs.at[1], sib)
    q_own[1 - zl] = q_part(k, 1 - zl)
    arrive(q_in.at[zl], qs_ss.at[0], qs_rs.at[0])
    arrive(q_in.at[1 - zl], qs_ss.at[1], qs_rs.at[1])
    q_send[...] = (q_own[...] + q_in[...]).astype(BF)
    for j, d in enumerate(DELTAS):
        px, pz = peer(*d)
        p = place(px, pz)
        send(q_send.at[p[0], p[1]], q_recv.at[j], q_ss.at[j], q_rs.at[j], dev(x=px, zh=pz))

    def gi_tile(n, _):
        cols = pl.ds(pl.multiple_of(n * 256, 256), 256)
        gi_v[:, cols] = dot(li_t[...], hid_all[:, :, :, :, cols].reshape(TOK, 256), 1, 0)
        return _

    lax.fori_loop(0, 3, gi_tile, 0)
    store_gi = pltpu.make_async_copy(gi_v, gi_out, loc.at[3])
    store_gi.start()

    total = q_own[mine[0], mine[1]] + q_in[mine[0], mine[1]]
    for j in range(len(DELTAS)):
        arrive(q_recv.at[j], q_ss.at[j], q_rs.at[j])
        total = total + q_recv[j].astype(F32)
    ig_out[...] = total.astype(BF)
    for c in started:
        c.wait_send()
    store_go.wait()
    store_gi.wait()


def on_device(layer_input, output_grad, preact, weight_in, weight_out):
    vmem, hbm = pl.BlockSpec(memory_space=pltpu.VMEM), pl.BlockSpec(memory_space=pl.ANY)
    dma = pltpu.SemaphoreType.DMA
    n = len(DELTAS)
    return pl.pallas_call(
        kernel,
        out_shape=(
            jax.ShapeDtypeStruct((T, DB), BF),
            jax.ShapeDtypeStruct((DB, FB), F32),
            jax.ShapeDtypeStruct((FB, DB), F32),
        ),
        in_specs=[vmem, vmem, vmem, hbm, hbm],
        out_specs=(vmem, hbm, hbm),
        scratch_shapes=[
            pltpu.VMEM((DB, FB), BF),
            pltpu.VMEM((FB, DB), BF),
            pltpu.VMEM((2, 2, 8, T, DB), BF),
            pltpu.VMEM((2, 2, 8, T, DB), BF),
            pltpu.VMEM((2, 2, 8, T, FB), BF),
            pltpu.VMEM((2, 2, 8, T, FB), BF),
            pltpu.VMEM((DB, TOK), BF),
            pltpu.VMEM((2, T, FB), F32),
            pltpu.VMEM((2, 8, T, FB), F32),
            pltpu.VMEM((2, 8, T, FB), BF),
            pltpu.VMEM((2, 8, T, FB), BF),
            pltpu.VMEM((2, 4, 2, T, FB), BF),
            pltpu.VMEM((2, 4, 2, T, FB), BF),
            pltpu.VMEM((2, 8, T, DB), F32),
            pltpu.VMEM((2, 8, T, DB), F32),
            pltpu.VMEM((2, 8, T, DB), F32),
            pltpu.VMEM((2, 8, T, DB), BF),
            pltpu.VMEM((n, T, DB), BF),
            pltpu.VMEM((DB, FB), F32),
            pltpu.VMEM((FB, DB), F32),
            dma((n,)), dma((n,)), dma, dma, dma((n,)), dma((n,)), dma, dma,
            dma((2, 4, 2)), dma((2, 4, 2)), dma((8, 2)), dma((8, 2)),
            dma((2, 4, 2)), dma((2, 4, 2)), dma((8, 2)), dma((8, 2)),
            dma((8, 2)), dma((8, 2)), dma((2, 4, 2)), dma((2, 4, 2)),
            dma((2,)), dma((2,)), dma((n,)), dma((n,)), dma((4,)),
        ],
        compiler_params=pltpu.CompilerParams(collective_id=0, has_side_effects=True, vmem_limit_bytes=48 * 2**20),
        cost_estimate=pl.CostEstimate(flops=8 * TOK * DB * FB, bytes_accessed=4 * 2**20, transcendentals=2 * 64 * FB),
        name="mlp_backward",
    )(layer_input, output_grad, preact, weight_in, weight_out)


def solution(mesh):
    in_specs = (P("row", "col"), P("row", "col"), P("col", "row"), P("col", "row"), P("row", "col"))
    out_specs = (P("row", "col"), P("col", "row"), P("row", "col"))
    return jax.shard_map(on_device, mesh=mesh, in_specs=in_specs, out_specs=out_specs, check_vma=False)
```

time: 405 us -> 108 us (0.27)
  waiting for transfers between devices: 259 us -> 0 us
  blocking collectives: 113 us -> 0 us
  Pallas kernels: 0 us -> 99.8 us
  between operations: 13.8 us -> 0.65 us
  matrix products: 11.6 us -> 0 us
  local copies, waits for them, and re-layouts: 2.68 us -> 7.12 us
    reduce_scatter x2 -> x0, waiting for transfers between devices: 182 us -> none  [the longest x1 107 us: on_device(): lax.psum_scatter(last_dims(rows, weight_in), 'row', scatter_dimension=0,...]
    all_gather x2 -> x0, blocking collectives: 113 us -> none  [the longest x1 58.6 us: on_device(): lax.all_gather(layer_input, 'row', axis=0, tiled=True)]
    pallas_call x0 -> x1, Pallas kernels: none -> 99.8 us  [on_device(): pl.pallas_call(kernel, out_shape=(jax.ShapeDtypeStruct((T, DB), BF), jax....]
    all_gather x2 -> x0, waiting for transfers between devices: 76.9 us -> none  [the longest x1 66.5 us: on_device(): lax.all_gather(hid_grad, 'col', axis=0, tiled=True)]
    dot_general x4 -> x0, matrix products: 11.6 us -> none  [the longest x2 6.19 us: last_dims(): lax.dot_general(left, right, (((1,), (1,)), ((), ())), preferred_element_...]
    unnamed x9 -> x13, local copies, waits for them, and re-layouts: 2.68 us -> 7.12 us
  transfers between devices with their start and end apart: 4 -> 0, of which waited for: 4 -> 0; matrix products, arithmetic and copies ran while one was open for 3% -> 0% of each run, Pallas kernels for 0% -> 0%
where the time goes in v1:
time: 108 us
  Pallas kernels  99.8 us (92%)
  local copies, waits for them, and re-layouts  7.12 us (7%)
    pallas_call x1, Pallas kernels, on_device(): pl.pallas_call(kernel, out_shape=(jax.ShapeDtypeStruct((T, DB), BF), jax....  99.8 us
    unnamed x13, local copies, waits for them, and re-layouts  7.12 us

profile of v1, /device:TPU:1, one launch (start us, length us, event | category | flops | bytes accessed | tf_op | source)
XLA Modules:
  0.0 107.5 jit_solution(4746238847589106832)
XLA Ops:
  0.6 0.0 copy-start
  0.6 1.1 copy-done
  1.7 0.0 copy-start.1
  1.7 1.1 copy-done.1
  2.8 0.0 copy-start.2
  2.8 0.9 copy-done.2
  3.7 0.0 copy-start.3
  3.7 0.7 copy-done.3
  4.4 0.0 copy-start.4
  4.4 0.7 copy-done.4
  5.1 99.8 %mlp_backward.1 = (bf16[32,384]{1,0:T(8,128)(2,1)S(1)}, f32[384,768]{1,0:T(8,128)S(1)}, f32[768,384]{1,0:T(8,128)S(1)}) custom-call(bf16[32,384]{1,0:T(8,128)(2,1)S(1)} %copy-done.3, bf16[32,384]{1,0:T(8,128)(2,1)S(1)} %copy-done.4, bf16[64,768]{1,0:T(8,128)(2,1)S(1)} %copy-done.2, bf16[384,768]{1,0:T(8,128)(2,1)S(1)} %copy-done, bf16[768,384]{1,0:T(8,128)(2,1)S(1)} %copy-done.1), custom_call_target="tpu_custom_call" | custom-call | flops 2415919104 | bytes 4194304 | tf_op jit(solution)/shard_map/mlp_backward/pallas_call | solution.py:264
  104.9 0.6 copy.11
  105.5 1.0 copy.12
  106.5 1.0 copy.13
Async XLA Ops:
  0.6 1.1 copy-start
  1.7 1.1 copy-start.1
  2.8 0.9 copy-start.2
  3.7 0.7 copy-start.3
  4.4 0.7 copy-start.4

commit v2 on v0

v2 whole, which is shorter than its diff:
```python
import math

import jax
import jax.numpy as jnp
from jax import lax
from jax.experimental import pallas as pl
from jax.experimental.pallas import tpu as pltpu
from jax.sharding import PartitionSpec as P

MESH = pl.DeviceIdType.MESH
BF, F32 = jnp.bfloat16, jnp.float32
TOK, DB, FB = 1024, 384, 768
T = 32
FT = 256


def gelu_parts(pre):
    cdf = 0.5 * (1.0 + lax.erf(pre * (1.0 / math.sqrt(2.0))))
    pdf = jnp.exp(-0.5 * pre * pre) * (1.0 / math.sqrt(2.0 * math.pi))
    return pre * cdf, cdf + pre * pdf


def dot(a, b, ca, cb):
    return lax.dot_general(a, b, (((ca,), (cb,)), ((), ())), preferred_element_type=F32)


def kernel(
    li, og, pre, w_in_hbm, w_out_hbm, ig_out, gi_out, go_out,
    li_v, og_v, pre_v, ig_v, w_in, w_out, og2, li_all, og_all, act_all, hid_all, li_t, slope, c_own, r_send, r_recv,
    q_sib, q_in, q_send, q_recv, q_self, gi_v, go_v,
    gz_ss, gz_rs, gx_ss, gx_rs, gs_ss, gs_rs, oz_ss, oz_rs, ox_ss, ox_rs, os_ss, os_rs, lz_ss, lz_rs, lx_ss, lx_rs, ls_ss, ls_rs,
    az_ss, az_rs, ay_ss, ay_rs, hy_ss, hy_rs, hz_ss, hz_rs, wo_ss, wo_rs, wi_ss, wi_rs, rr_ss, rr_rs,
    qs_ss, qs_rs, q_ss, q_rs, loc,
):
    row, col = lax.axis_index("row"), lax.axis_index("col")
    x, zh, k = row // 8, (row // 2) % 4, row % 2
    y, zl = col // 2, col % 2
    halves = (1 - k, k)
    my = 2 * x + zh // 2
    same = zh % 2 == zl
    odd = (zh + zl) % 2

    def dev(x=x, zh=zh, k=k, y=y, zl=zl):
        return (x * 8 + zh * 2 + k, y * 2 + zl)

    sib, zpart = dev(k=1 - k), dev(zl=1 - zl)
    ynext = [dev(y=(y + 1) % 8), dev(y=(y + 7) % 8)]
    started = []

    def send(src, dst, ss, rs, to, cond=None):
        c = pltpu.make_async_remote_copy(src_ref=src, dst_ref=dst, send_sem=ss, recv_sem=rs, device_id=to, device_id_type=MESH)
        if cond is None:
            c.start()
        else:
            pl.when(cond)(c.start)
        started.append((cond, c))

    def arrive(dst, ss, rs):
        pltpu.make_async_remote_copy(src_ref=dst, dst_ref=dst, send_sem=ss, recv_sem=rs, device_id=sib, device_id_type=MESH).wait_recv()

    loads = [
        pltpu.make_async_copy(a, b, loc.at[i])
        for i, (a, b) in enumerate([(og, og_v), (pre, pre_v), (w_out_hbm, w_out.at[zl]), (w_in_hbm, w_in.at[zl]), (li, li_v)])
    ]
    for c in loads:
        c.start()

    barrier = pltpu.get_barrier_semaphore()
    greet = [dev(zh=(zh + a) % 4, zl=(zl + b) % 2) for a in range(4) for b in range(2) if (a, b) != (0, 0)]
    greet += [dev(x=(x + a) % 4, k=c) for a in (1, 2, 3) for c in (k, 1 - k)] + ynext + [sib]
    greet += [dev(x=(x + a) % 4, zh=b, zl=zh % 2) for a in (1, 2, 3) for b in range(4)]
    for p in greet:
        pl.semaphore_signal(barrier, inc=1, device_id=p, device_id_type=MESH)
    loads[0].wait()
    pl.semaphore_wait(barrier, len(greet))

    for dz in (2, 1, 3):
        send(og_v, og2.at[zl, k, my], gz_ss.at[dz], gz_rs.at[zl, dz], dev(zh=(zh + dz) % 4, zl=zh % 2))
    send(og_v, og2.at[zl, k, my], gz_ss.at[0], gz_rs.at[zl, 0], dev(zl=zh % 2), jnp.logical_not(same))

    @pl.when(same)
    def _():
        og2[zl, k, my] = og_v[...]

    for n in range(3):
        rows = pl.ds(n * FT, FT)
        send(w_out_hbm.at[rows], w_out.at[zl, rows], wo_ss.at[n], wo_rs.at[n], zpart)

    loads[1].wait()
    for h in range(2):
        value, sl = gelu_parts(pre_v[pl.ds(h * T, T), :].astype(F32))
        act_all[zl, h, y] = value.astype(BF)
        slope[h] = sl

    def act_step(j, s):
        zz = zl if j == 0 else 1 - zl
        for h in range(2):
            if s == 0 and j == 0:
                ref = act_all.at[zl, h, y]
                send(ref, ref, az_ss.at[h], az_rs.at[h], zpart)
            if s == 0 and j == 1:
                arrive(act_all.at[zz, h, y], az_ss.at[h], az_rs.at[h])
            for d in range(2):
                hops = 4 if h == d else 3
                ref = act_all.at[zz, h, (y + (8 - s if d == 0 else s)) % 8]
                if 0 < s <= hops:
                    arrive(ref, ay_ss.at[j, d, s - 1, h], ay_rs.at[j, d, s - 1, h])
                if s < hops:
                    send(ref, ref, ay_ss.at[j, d, s, h], ay_rs.at[j, d, s, h], ynext[d])

    act_step(0, 0)

    def source(e):
        dz = 2 * e + odd
        return dz, (zh + 4 - dz) % 4 // 2

    for e in range(2):
        for zs in range(2):
            dz, p = source(e)
            ref = og2.at[zs, k, 2 * x + p]
            if e == 0:

                @pl.when(jnp.logical_not(same & (zl == zs)))
                def _():
                    arrive(ref, gz_ss.at[0], gz_rs.at[zs, dz])

            else:
                arrive(ref, gz_ss.at[0], gz_rs.at[zs, dz])
            for dx in (2, 1, 3, 0):
                send(ref, ref, gx_ss.at[dx, e, zs], gx_rs.at[dx, e, zs], dev(x=(x + dx) % 4, k=1 - k))
    act_step(1, 0)
    act_step(0, 1)

    for dx in (0, 1, 3, 2):
        xs = (x + 4 - dx) % 4
        for zs in range(2):
            for e in range(2):
                arrive(og2.at[zs, 1 - k, 2 * xs + source(e)[1]], gx_ss.at[dx, e, zs], gx_rs.at[dx, e, zs])
            if dx > 0:
                ref = og2.at[zs, 1 - k, pl.ds(2 * xs, 2)]
                send(ref, ref, gs_ss.at[dx - 1, zs], gs_rs.at[dx - 1, zs], sib)
    act_step(1, 1)
    act_step(0, 2)

    loads[2].wait()

    def partial(a):
        h = halves[a]
        for n in range(3):
            rows = pl.ds(n * FT, FT)
            if a == 0:
                arrive(w_out.at[1 - zl, rows], wo_ss.at[n], wo_rs.at[n])
            total = dot(og2[0, h].reshape(8 * T, DB), w_out[0, rows, :], 1, 1)
            total += dot(og2[1, h].reshape(8 * T, DB), w_out[1, rows, :], 1, 1)
            c_own[h, :, :, rows] = total.reshape(8, T, FT)

    def rs_step(a, s):
        h = halves[a]
        for d in range(2):
            hops = 4 if a == d else 3
            if s >= hops:
                continue
            to = hops - s
            total = c_own[h, (y + (to if d == 0 else 8 - to)) % 8]
            if s > 0:
                arrive(r_recv.at[d, s - 1, a], rr_ss.at[d, s - 1, a], rr_rs.at[d, s - 1, a])
                total = total + r_recv[d, s - 1, a].astype(F32)
            r_send[d, s, a] = total.astype(BF)
            send(r_send.at[d, s, a], r_recv.at[d, s, a], rr_ss.at[d, s, a], rr_rs.at[d, s, a], ynext[d])

    def rs_last(a):
        h = halves[a]
        total = c_own[h, y]
        for d in range(2):
            s = 3 if a == d else 2
            arrive(r_recv.at[d, s, a], rr_ss.at[d, s, a], rr_rs.at[d, s, a])
            total = total + r_recv[d, s, a].astype(F32)
        hid_all[zl, h, y] = (total * slope[h]).astype(BF)

    def in_z(own, full, ss, rs):
        full[zh % 2, k, my] = own[...]
        for dz in (2, 1, 3):
            send(own, full.at[zh % 2, k, my], ss.at[dz - 1], rs.at[dz - 1], dev(zh=(zh + dz) % 4))

    def in_x(full, zss, zrs, ss, rs):
        for dz in (0, 1, 3, 2):
            zs = (zh + 4 - dz) % 4
            ref = full.at[zs % 2, k, 2 * x + zs // 2]
            if dz > 0:
                arrive(ref, zss.at[dz - 1], zrs.at[dz - 1])
            for dx in (2, 1, 3):
                send(ref, ref, ss.at[dx - 1, dz], rs.at[dx - 1, dz], dev(x=(x + dx) % 4))

    def in_core(full, xss, xrs, ss, rs):
        for dx in (1, 3, 2):
            for dz in range(4):
                xs, zs = (x + 4 - dx) % 4, (zh + 4 - dz) % 4
                arrive(full.at[zs % 2, k, 2 * xs + zs // 2], xss.at[dx - 1, dz], xrs.at[dx - 1, dz])
        for b in range(2):
            send(full.at[b, k], full.at[b, k], ss.at[b], rs.at[b], sib)

    def in_done(full, ss, rs):
        for b in range(2):
            arrive(full.at[b, 1 - k], ss.at[b], rs.at[b])

    partial(0)
    rs_step(0, 0)
    act_step(1, 2)
    act_step(0, 3)
    for dx in (1, 3, 2):
        for zs in range(2):
            ref = og2.at[zs, k, pl.ds(2 * ((x + 4 - dx) % 4), 2)]
            arrive(ref, gs_ss.at[dx - 1, zs], gs_rs.at[dx - 1, zs])
    partial(1)
    rs_step(1, 0)
    send(w_in_hbm, w_in.at[zl], wi_ss, wi_rs, zpart)
    loads[4].wait()
    in_z(og_v, og_all, oz_ss, oz_rs)
    in_z(li_v, li_all, lz_ss, lz_rs)
    act_step(1, 3)
    rs_step(0, 1)
    rs_step(1, 1)
    act_step(0, 4)
    act_step(1, 4)
    in_x(og_all, oz_ss, oz_rs, ox_ss, ox_rs)
    rs_step(0, 2)
    rs_step(1, 2)
    in_x(li_all, lz_ss, lz_rs, lx_ss, lx_rs)
    rs_step(0, 3)
    rs_step(1, 3)
    in_core(og_all, ox_ss, ox_rs, os_ss, os_rs)

    def ag_step(a, s):
        h = halves[a]
        for d in range(2):
            hops = 4 if a == d else 3
            off = (8 - s) % 8 if d == 0 else s
            ref = hid_all.at[zl, h, (y + off) % 8]
            if 0 < s <= hops:
                arrive(ref, hy_ss.at[d, s - 1, a], hy_rs.at[d, s - 1, a])
            if s < hops:
                send(ref, ref, hy_ss.at[d, s, a], hy_rs.at[d, s, a], ynext[d])
            if s <= hops and (s > 0 or d == 0):
                send(ref, ref, hz_ss.at[off, a], hz_rs.at[off, a], zpart)

    def q_part(a, offs):
        at = [(y + o) % 8 for o in offs]
        rows = jnp.concatenate([hid_all[zl, halves[a], p] for p in at], axis=0)
        for zs in range(2):
            q = dot(rows, w_in[zs], 1, 1)
            for i, (o, p) in enumerate(zip(offs, at, strict=True)):
                part = q[i * T : (i + 1) * T]
                if a == 0:
                    q_sib[p, zs] = part
                    if zs == 1:
                        send(q_sib.at[p], q_in.at[p], qs_ss.at[o], qs_rs.at[o], sib)
                    continue
                if zs == 0:
                    arrive(q_in.at[p], qs_ss.at[o], qs_rs.at[o])
                part = part + q_in[p, zs]
                q_send[p, zs] = part.astype(BF)
                mine = (p == my) & same & (zl == zs)

                @pl.when(mine)
                def _():
                    q_self[...] = part

                px, pz = p // 2, 2 * (p % 2) + zl
                slot = (px + 4 - x) % 4 * 4 + (pz + 4 - zh) % 4
                send(q_send.at[p, zs], q_recv.at[slot], q_ss.at[o, zs], q_rs.at[slot], dev(x=px, zh=pz, zl=zs), jnp.logical_not(mine))

    def go_tile(n):
        cols = pl.ds(n * FT, FT)
        go_v[cols, :] = dot(act_all[:, :, :, :, cols].reshape(TOK, FT), og_all[...].reshape(TOK, DB), 0, 0)

    rs_last(0)
    ag_step(0, 0)
    rs_last(1)
    ag_step(1, 0)
    in_core(li_all, lx_ss, lx_rs, ls_ss, ls_rs)
    ag_step(0, 1)
    ag_step(1, 1)
    loads[3].wait()
    arrive(w_in.at[1 - zl], wi_ss, wi_rs)
    q_part(0, (0, 1, 7))
    q_part(1, (0, 1, 7))
    ag_step(0, 2)
    ag_step(1, 2)
    q_part(0, (2, 6))
    q_part(1, (2, 6))
    ag_step(0, 3)
    ag_step(1, 3)
    q_part(0, (3, 5))
    q_part(1, (3, 5))
    ag_step(0, 4)
    q_part(0, (4,))
    ag_step(1, 4)
    q_part(1, (4,))
    in_done(og_all, os_ss, os_rs)
    for n in range(3):
        go_tile(n)
    store_go = pltpu.make_async_copy(go_v, go_out, loc.at[5])
    store_go.start()
    in_done(li_all, ls_ss, ls_rs)
    li_t[...] = li_all[...].reshape(TOK, DB).T
    for o in range(8):
        for a in range(2):
            arrive(hid_all.at[1 - zl, halves[a], (y + o) % 8], hz_ss.at[o, a], hz_rs.at[o, a])
    for n in range(3):
        cols = pl.ds(n * FT, FT)
        gi_v[:, cols] = dot(li_t[...], hid_all[:, :, :, :, cols].reshape(TOK, FT), 1, 0)
    store_gi = pltpu.make_async_copy(gi_v, gi_out, loc.at[6])
    store_gi.start()
    @pl.when(jnp.logical_not(same))
    def _():
        arrive(q_recv.at[0], q_ss.at[0, 0], q_rs.at[0])
        q_self[...] = q_recv[0].astype(F32)

    total = q_self[...]
    for j in range(1, 16):
        arrive(q_recv.at[j], q_ss.at[0, 0], q_rs.at[j])
        total = total + q_recv[j].astype(F32)
    ig_v[...] = total.astype(BF)
    store_ig = pltpu.make_async_copy(ig_v, ig_out, loc.at[7])
    store_ig.start()
    for cond, c in started:
        if cond is None:
            c.wait_send()
        else:
            pl.when(cond)(c.wait_send)
    store_go.wait()
    store_gi.wait()
    store_ig.wait()


def on_device(layer_input, output_grad, preact, weight_in, weight_out):
    hbm = pl.BlockSpec(memory_space=pl.ANY)
    vmem, dma = pltpu.VMEM, pltpu.SemaphoreType.DMA
    sems = [
        ((4,), (2, 4)), ((4, 2, 2), (4, 2, 2)), ((3, 2), (3, 2)),
        ((3,), (3,)), ((3, 4), (3, 4)), ((2,), (2,)), ((3,), (3,)), ((3, 4), (3, 4)), ((2,), (2,)),
        ((2,), (2,)), ((2, 2, 4, 2), (2, 2, 4, 2)), ((2, 4, 2), (2, 4, 2)), ((8, 2), (8, 2)),
        ((3,), (3,)), (None, None), ((2, 4, 2), (2, 4, 2)), ((8,), (8,)), ((8, 2), (16,)),
    ]
    return pl.pallas_call(
        kernel,
        out_shape=(
            jax.ShapeDtypeStruct((T, DB), BF),
            jax.ShapeDtypeStruct((DB, FB), F32),
            jax.ShapeDtypeStruct((FB, DB), F32),
        ),
        in_specs=[hbm] * 5,
        out_specs=(hbm, hbm, hbm),
        scratch_shapes=[
            vmem((T, DB), BF),
            vmem((T, DB), BF),
            vmem((2 * T, FB), BF),
            vmem((T, DB), BF),
            vmem((2, DB, FB), BF),
            vmem((2, FB, DB), BF),
            vmem((2, 2, 8, T, DB), BF),
            vmem((2, 2, 8, T, DB), BF),
            vmem((2, 2, 8, T, DB), BF),
            vmem((2, 2, 8, T, FB), BF),
            vmem((2, 2, 8, T, FB), BF),
            vmem((DB, TOK), BF),
            vmem((2, T, FB), F32),
            vmem((2, 8, T, FB), F32),
            vmem((2, 4, 2, T, FB), BF),
            vmem((2, 4, 2, T, FB), BF),
            vmem((8, 2, T, DB), F32),
            vmem((8, 2, T, DB), F32),
            vmem((8, 2, T, DB), BF),
            vmem((16, T, DB), BF),
            vmem((T, DB), F32),
            vmem((DB, FB), F32),
            vmem((FB, DB), F32),
        ]
        + [dma if s is None else dma(s) for pair in sems for s in pair]
        + [dma((8,))],
        compiler_params=pltpu.CompilerParams(collective_id=0, has_side_effects=True, vmem_limit_bytes=60 * 2**20),
        cost_estimate=pl.CostEstimate(flops=8 * TOK * DB * FB, bytes_accessed=4 * 2**20, transcendentals=2 * 64 * FB),
        name="mlp_backward",
    )(layer_input, output_grad, preact, weight_in, weight_out)


def solution(mesh):
    in_specs = (P("row", "col"), P("row", "col"), P("col", "row"), P("col", "row"), P("row", "col"))
    out_specs = (P("row", "col"), P("col", "row"), P("row", "col"))
    return jax.shard_map(on_device, mesh=mesh, in_specs=in_specs, out_specs=out_specs, check_vma=False)
```

time: 405 us -> 107 us (0.26)
  waiting for transfers between devices: 259 us -> 0 us
  blocking collectives: 113 us -> 0 us
  Pallas kernels: 0 us -> 101 us
  between operations: 13.8 us -> 0.64 us
  matrix products: 11.6 us -> 0 us
    reduce_scatter x2 -> x0, waiting for transfers between devices: 182 us -> none  [the longest x1 107 us: on_device(): lax.psum_scatter(last_dims(rows, weight_in), 'row', scatter_dimension=0,...]
    all_gather x2 -> x0, blocking collectives: 113 us -> none  [the longest x1 58.6 us: on_device(): lax.all_gather(layer_input, 'row', axis=0, tiled=True)]
    pallas_call x0 -> x1, Pallas kernels: none -> 101 us  [on_device(): pl.pallas_call(kernel, out_shape=(jax.ShapeDtypeStruct((T, DB), BF), jax....]
    all_gather x2 -> x0, waiting for transfers between devices: 76.9 us -> none  [the longest x1 66.5 us: on_device(): lax.all_gather(hid_grad, 'col', axis=0, tiled=True)]
    dot_general x4 -> x0, matrix products: 11.6 us -> none  [the longest x2 6.19 us: last_dims(): lax.dot_general(left, right, (((1,), (1,)), ((), ())), preferred_element_...]
  transfers between devices with their start and end apart: 4 -> 0, of which waited for: 4 -> 0; matrix products, arithmetic and copies ran while one was open for 3% -> 0% of each run, Pallas kernels for 0% -> 0%
where the time goes in v2:
time: 107 us; the launch traced here: 106 us
  Pallas kernels  101 us (94%)
  local copies, waits for them, and re-layouts  4.82 us (5%)
    pallas_call x1, Pallas kernels, on_device(): pl.pallas_call(kernel, out_shape=(jax.ShapeDtypeStruct((T, DB), BF), jax....  101 us
    unnamed x5, local copies, waits for them, and re-layouts  4.82 us

profile of v2, /device:TPU:1, one launch (start us, length us, event | category | flops | bytes accessed | tf_op | source)
XLA Modules:
  0.0 106.0 jit_solution(2310130584327456671)
XLA Ops:
  0.6 100.6 %mlp_backward.1 = (bf16[32,384]{1,0:T(8,128)(2,1)}, f32[384,768]{1,0:T(8,128)}, f32[768,384]{1,0:T(8,128)}) custom-call(bf16[32,384]{1,0:T(8,128)(2,1)} %li.1, bf16[32,384]{1,0:T(8,128)(2,1)} %og.1, bf16[64,768]{1,0:T(8,128)(2,1)} %pre.1, bf16[384,768]{1,0:T(8,128)(2,1)} %w_in_hbm.1, bf16[768,384]{1,0:T(8,128)(2,1)} %w_out_hbm.1), custom_call_target="tpu_custom_call" | custom-call | flops 2415919104 | bytes 4194304 | tf_op jit(solution)/shard_map/mlp_backward/pallas_call | solution.py:345
  101.2 1.3 %copy.11 = bf16[32,384]{1,0:T(8,128)(2,1)} copy(bf16[32,384]{1,0:T(8,128)(2,1)} %get-tuple-element.6) | data formatting | bytes 49152
  102.6 0.0 copy-start
  102.6 2.5 %copy.12 = f32[384,768]{1,0:T(8,128)} copy(f32[384,768]{1,0:T(8,128)} %get-tuple-element.7) | data formatting | bytes 2359296
  105.0 0.0 copy-done
  105.0 1.0 copy.13
Async XLA Ops:
  102.6 2.5 %copy-start = (f32[768,384]{1,0:T(8,128)S(1)}, f32[768,384]{1,0:T(8,128)}, u32[]{:S(2)}) copy-start(f32[768,384]{1,0:T(8,128)} %get-tuple-element.8) | copy-start | bytes 3538948

commit v3 on v2

v3 whole, which is shorter than its diff:
```python
import math

import jax
import jax.numpy as jnp
from jax import lax
from jax.experimental import pallas as pl
from jax.experimental.pallas import tpu as pltpu
from jax.sharding import PartitionSpec as P

MESH = pl.DeviceIdType.MESH
BF, F32 = jnp.bfloat16, jnp.float32
TOK, DB, FB = 1024, 384, 768
T = 32
FT = 256
FA = 512


def gelu_parts(pre):
    cdf = 0.5 * (1.0 + lax.erf(pre * (1.0 / math.sqrt(2.0))))
    pdf = jnp.exp(-0.5 * pre * pre) * (1.0 / math.sqrt(2.0 * math.pi))
    return pre * cdf, cdf + pre * pdf


def dot(a, b, ca, cb):
    return lax.dot_general(a, b, (((ca,), (cb,)), ((), ())), preferred_element_type=F32)


def kernel(
    li, og, pre, w_in_hbm, w_out_hbm, ig_out, gi_out, go_out,
    li_v, og_v, pre_v, w_in, w_out, li_all, og_all, act_all, hid_all, li_t, slope, c_a, c_b, cz_send, cz_recv,
    ra_send, ra_recv, rb_send, rb_recv, bz_send, bz_recv, q_sib, q_in, q_send, q_recv, q_self,
    oz_ss, oz_rs, ox_ss, ox_rs, os_ss, os_rs, lz_ss, lz_rs, lx_ss, lx_rs, ls_ss, ls_rs,
    az_ss, az_rs, ay_ss, ay_rs, hy_ss, hy_rs, hz_ss, hz_rs, wi_ss, wi_rs, cz_ss, cz_rs, ra_ss, ra_rs, rb_ss, rb_rs, bz_ss, bz_rs,
    qs_ss, qs_rs, q_ss, q_rs, loc,
):
    row, col = lax.axis_index("row"), lax.axis_index("col")
    x, zh, k = row // 8, (row // 2) % 4, row % 2
    y, zl = col // 2, col % 2
    halves = (1 - k, k)
    my = 2 * x + zh // 2
    same = zh % 2 == zl

    def dev(x=x, zh=zh, k=k, y=y, zl=zl):
        return (x * 8 + zh * 2 + k, y * 2 + zl)

    sib, zpart = dev(k=1 - k), dev(zl=1 - zl)
    ynext = [dev(y=(y + 1) % 8), dev(y=(y + 7) % 8)]
    started = []

    def send(src, dst, ss, rs, to, cond=None):
        c = pltpu.make_async_remote_copy(src_ref=src, dst_ref=dst, send_sem=ss, recv_sem=rs, device_id=to, device_id_type=MESH)
        if cond is None:
            c.start()
        else:
            pl.when(cond)(c.start)
        started.append((cond, c))

    def arrive(dst, ss, rs):
        pltpu.make_async_remote_copy(src_ref=dst, dst_ref=dst, send_sem=ss, recv_sem=rs, device_id=sib, device_id_type=MESH).wait_recv()

    loads = [
        pltpu.make_async_copy(a, b, loc.at[i])
        for i, (a, b) in enumerate([(og, og_v), (pre, pre_v), (w_out_hbm, w_out), (w_in_hbm, w_in.at[zl]), (li, li_v)])
    ]
    for c in loads:
        c.start()

    barrier = pltpu.get_barrier_semaphore()
    greet = [dev(zh=(zh + a) % 4, zl=(zl + b) % 2) for a in range(4) for b in range(2) if (a, b) != (0, 0)]
    greet += [dev(x=(x + a) % 4, k=c) for a in (1, 2, 3) for c in (k, 1 - k)] + ynext + [sib]
    greet += [dev(x=(x + a) % 4, zh=b, zl=zh % 2) for a in (1, 2, 3) for b in range(4)]
    for p in greet:
        pl.semaphore_signal(barrier, inc=1, device_id=p, device_id_type=MESH)
    loads[0].wait()
    pl.semaphore_wait(barrier, len(greet))

    def in_z(own, full, ss, rs):
        full[zh % 2, k, my] = own[...]
        for dz in (2, 1, 3):
            send(own, full.at[zh % 2, k, my], ss.at[dz - 1], rs.at[dz - 1], dev(zh=(zh + dz) % 4))

    def in_x(full, zss, zrs, ss, rs):
        for dz in (0, 1, 3, 2):
            zs = (zh + 4 - dz) % 4
            ref = full.at[zs % 2, k, 2 * x + zs // 2]
            if dz > 0:
                arrive(ref, zss.at[dz - 1], zrs.at[dz - 1])
            for dx in (2, 1, 3, 0):
                send(ref, ref, ss.at[dx, dz], rs.at[dx, dz], dev(x=(x + dx) % 4, k=1 - k))

    def in_core(full, xss, xrs, ss, rs):
        for dx in (0, 1, 3, 2):
            xs = (x + 4 - dx) % 4
            for dz in range(4):
                zs = (zh + 4 - dz) % 4
                arrive(full.at[zs % 2, 1 - k, 2 * xs + zs // 2], xss.at[dx, dz], xrs.at[dx, dz])
            if dx > 0:
                for b in range(2):
                    ref = full.at[b, 1 - k, pl.ds(2 * xs, 2)]
                    send(ref, ref, ss.at[dx - 1, b], rs.at[dx - 1, b], sib)

    def in_done(full, ss, rs):
        for dx in (1, 3, 2):
            for b in range(2):
                arrive(full.at[b, k, pl.ds(2 * ((x + 4 - dx) % 4), 2)], ss.at[dx - 1, b], rs.at[dx - 1, b])

    in_z(og_v, og_all, oz_ss, oz_rs)
    loads[1].wait()
    for h in range(2):
        value, sl = gelu_parts(pre_v[pl.ds(h * T, T), :].astype(F32))
        act_all[zl, h, y] = value.astype(BF)
        slope[h] = sl

    def act_step(j, s):
        zz = zl if j == 0 else 1 - zl
        for h in range(2):
            if s == 0 and j == 0:
                ref = act_all.at[zl, h, y]
                send(ref, ref, az_ss.at[h], az_rs.at[h], zpart)
            if s == 0 and j == 1:
                arrive(act_all.at[zz, h, y], az_ss.at[h], az_rs.at[h])
            for d in range(2):
                hops = 4 if h == d else 3
                ref = act_all.at[zz, h, (y + (8 - s if d == 0 else s)) % 8]
                if 0 < s <= hops:
                    arrive(ref, ay_ss.at[j, d, s - 1, h], ay_rs.at[j, d, s - 1, h])
                if s < hops:
                    send(ref, ref, ay_ss.at[j, d, s, h], ay_rs.at[j, d, s, h], ynext[d])

    act_step(0, 0)
    in_x(og_all, oz_ss, oz_rs, ox_ss, ox_rs)
    send(w_in_hbm, w_in.at[zl], wi_ss, wi_rs, zpart)
    act_step(0, 1)
    in_core(og_all, ox_ss, ox_rs, os_ss, os_rs)
    act_step(1, 0)

    def partial(half, a, n):
        return dot(og_all[half, halves[a]].reshape(8 * T, DB), w_out[pl.ds(n * FT, FT), :], 1, 1).reshape(8, T, FT)

    def partials(a):
        h = halves[a]
        for n in (1, 2):
            cz_send[h, :, :, pl.ds(n * FT - FT, FT)] = partial(1 - zl, a, n).astype(BF)
        for o in (4, 3, 5, 2, 6, 1, 7, 0):
            at = (y + o) % 8
            send(cz_send.at[h, at], cz_recv.at[h, at], cz_ss.at[o, a], cz_rs.at[o, a], zpart)
        for b in range(2):
            c_b[h, :, b] = partial(b, a, 0)
        rs_b(a, 0)
        for n in (1, 2):
            c_a[h, :, :, pl.ds(n * FT - FT, FT)] = partial(zl, a, n)

    def rs_b(a, s):
        h = halves[a]
        for d in range(2):
            hops = 3 if a == d else 4
            if s >= hops:
                continue
            to = hops - s
            total = c_b[h, (y + (to if d == 0 else 8 - to)) % 8]
            if s > 0:
                arrive(rb_recv.at[d, s - 1, a], rb_ss.at[d, s - 1, a], rb_rs.at[d, s - 1, a])
                total = total + rb_recv[d, s - 1, a].astype(F32)
            rb_send[d, s, a] = total.astype(BF)
            send(rb_send.at[d, s, a], rb_recv.at[d, s, a], rb_ss.at[d, s, a], rb_rs.at[d, s, a], ynext[d])

    def mine(a, o):
        h, at = halves[a], (y + o) % 8
        arrive(cz_recv.at[h, at], cz_ss.at[o, a], cz_rs.at[o, a])
        return c_a[h, at] + cz_recv[h, at].astype(F32)

    def rs_a(a, s):
        for d in range(2):
            hops = 4 if a == d else 3
            if s >= hops:
                continue
            to = hops - s
            total = mine(a, to if d == 0 else 8 - to)
            if s > 0:
                arrive(ra_recv.at[d, s - 1, a], ra_ss.at[d, s - 1, a], ra_rs.at[d, s - 1, a])
                total = total + ra_recv[d, s - 1, a].astype(F32)
            ra_send[d, s, a] = total.astype(BF)
            send(ra_send.at[d, s, a], ra_recv.at[d, s, a], ra_ss.at[d, s, a], ra_rs.at[d, s, a], ynext[d])

    def last_b(a):
        h = halves[a]
        for d in range(2):
            s = 2 if a == d else 3
            arrive(rb_recv.at[d, s, a], rb_ss.at[d, s, a], rb_rs.at[d, s, a])
        bz_send[a] = (c_b[h, y, 1 - zl] + rb_recv[0, 2 if a == 0 else 3, a, 1 - zl].astype(F32) + rb_recv[1, 2 if a == 1 else 3, a, 1 - zl].astype(F32)).astype(BF)
        send(bz_send.at[a], bz_recv.at[a], bz_ss.at[a], bz_rs.at[a], zpart)

    def last_a(a):
        h = halves[a]
        total = mine(a, 0)
        for d in range(2):
            s = 3 if a == d else 2
            arrive(ra_recv.at[d, s, a], ra_ss.at[d, s, a], ra_rs.at[d, s, a])
            total = total + ra_recv[d, s, a].astype(F32)
        hid_all[zl, h, y, :, pl.ds(FT, FA)] = (total * slope[h, :, pl.ds(FT, FA)]).astype(BF)
        total = c_b[h, y, zl] + rb_recv[0, 2 if a == 0 else 3, a, zl].astype(F32) + rb_recv[1, 2 if a == 1 else 3, a, zl].astype(F32)
        arrive(bz_recv.at[a], bz_ss.at[a], bz_rs.at[a])
        total = total + bz_recv[a].astype(F32)
        hid_all[zl, h, y, :, pl.ds(0, FT)] = (total * slope[h, :, pl.ds(0, FT)]).astype(BF)

    loads[2].wait()
    partials(0)
    act_step(1, 1)
    in_done(og_all, os_ss, os_rs)
    partials(1)
    rs_a(0, 0)
    rs_a(1, 0)
    act_step(0, 2)
    rs_b(0, 1)
    rs_b(1, 1)
    rs_a(0, 1)
    rs_a(1, 1)
    act_step(1, 2)
    rs_b(0, 2)
    rs_b(1, 2)
    rs_a(0, 2)
    rs_a(1, 2)
    rs_b(0, 3)
    rs_b(1, 3)
    rs_a(0, 3)
    rs_a(1, 3)
    act_step(0, 3)
    loads[4].wait()
    in_z(li_v, li_all, lz_ss, lz_rs)
    last_b(0)
    last_b(1)

    def ag_step(a, s):
        h = halves[a]
        for d in range(2):
            hops = 4 if a == d else 3
            off = (8 - s) % 8 if d == 0 else s
            ref = hid_all.at[zl, h, (y + off) % 8]
            if 0 < s <= hops:
                arrive(ref, hy_ss.at[d, s - 1, a], hy_rs.at[d, s - 1, a])
            if s < hops:
                send(ref, ref, hy_ss.at[d, s, a], hy_rs.at[d, s, a], ynext[d])
            if s <= hops and (s > 0 or d == 0):
                send(ref, ref, hz_ss.at[off, a], hz_rs.at[off, a], zpart)

    def q_part(a, offs):
        at = [(y + o) % 8 for o in offs]
        rows = jnp.concatenate([hid_all[zl, halves[a], p] for p in at], axis=0)
        for zs in range(2):
            q = dot(rows, w_in[zs], 1, 1)
            for i, (o, p) in enumerate(zip(offs, at, strict=True)):
                part = q[i * T : (i + 1) * T]
                if a == 0:
                    q_sib[p, zs] = part
                    if zs == 1:
                        send(q_sib.at[p], q_in.at[p], qs_ss.at[o], qs_rs.at[o], sib)
                    continue
                if zs == 0:
                    arrive(q_in.at[p], qs_ss.at[o], qs_rs.at[o])
                part = part + q_in[p, zs]
                q_send[p, zs] = part.astype(BF)
                stays = (p == my) & same & (zl == zs)

                @pl.when(stays)
                def _():
                    q_self[...] = part

                px, pz = p // 2, 2 * (p % 2) + zl
                slot = (px + 4 - x) % 4 * 4 + (pz + 4 - zh) % 4
                send(q_send.at[p, zs], q_recv.at[slot], q_ss.at[o, zs], q_rs.at[slot], dev(x=px, zh=pz, zl=zs), jnp.logical_not(stays))

    def go_tile(n):
        cols = pl.ds(n * FT, FT)
        go_out[cols, :] = dot(act_all[:, :, :, :, cols].reshape(TOK, FT), og_all[...].reshape(TOK, DB), 0, 0)

    last_a(0)
    ag_step(0, 0)
    last_a(1)
    ag_step(1, 0)
    act_step(1, 3)
    act_step(0, 4)
    in_x(li_all, lz_ss, lz_rs, lx_ss, lx_rs)
    ag_step(0, 1)
    ag_step(1, 1)
    loads[3].wait()
    arrive(w_in.at[1 - zl], wi_ss, wi_rs)
    q_part(0, (0, 1, 7))
    q_part(1, (0, 1, 7))
    act_step(1, 4)
    ag_step(0, 2)
    ag_step(1, 2)
    q_part(0, (2, 6))
    q_part(1, (2, 6))
    in_core(li_all, lx_ss, lx_rs, ls_ss, ls_rs)
    ag_step(0, 3)
    ag_step(1, 3)
    q_part(0, (3, 5))
    q_part(1, (3, 5))
    ag_step(0, 4)
    q_part(0, (4,))
    ag_step(1, 4)
    q_part(1, (4,))
    for n in range(3):
        go_tile(n)
    in_done(li_all, ls_ss, ls_rs)
    li_t[...] = li_all[...].reshape(TOK, DB).T
    for o in range(8):
        for a in range(2):
            arrive(hid_all.at[1 - zl, halves[a], (y + o) % 8], hz_ss.at[o, a], hz_rs.at[o, a])
    for n in range(3):
        cols = pl.ds(n * FT, FT)
        gi_out[:, cols] = dot(li_t[...], hid_all[:, :, :, :, cols].reshape(TOK, FT), 1, 0)
    @pl.when(jnp.logical_not(same))
    def _():
        arrive(q_recv.at[0], q_ss.at[0, 0], q_rs.at[0])
        q_self[...] = q_recv[0].astype(F32)

    total = q_self[...]
    for j in range(1, 16):
        arrive(q_recv.at[j], q_ss.at[0, 0], q_rs.at[j])
        total = total + q_recv[j].astype(F32)
    ig_out[...] = total.astype(BF)
    for cond, c in started:
        if cond is None:
            c.wait_send()
        else:
            pl.when(cond)(c.wait_send)


def on_device(layer_input, output_grad, preact, weight_in, weight_out):
    vmem, dma = pltpu.VMEM, pltpu.SemaphoreType.DMA
    ins = [pltpu.with_memory_space_constraint(a, pltpu.HBM) for a in (layer_input, output_grad, preact, weight_in, weight_out)]
    gather = [(3,), (3,), (4, 4), (4, 4), (3, 2), (3, 2)]
    sems = gather + gather
    sems += [s for s in [(2,), (2, 2, 4, 2), (2, 4, 2), (8, 2), None, (8, 2), (2, 4, 2), (2, 4, 2), (2,), (8,)] for _ in range(2)]
    sems += [(8, 2), (16,), (5,)]
    return pl.pallas_call(
        kernel,
        out_shape=(
            jax.ShapeDtypeStruct((T, DB), BF),
            jax.ShapeDtypeStruct((DB, FB), F32),
            jax.ShapeDtypeStruct((FB, DB), F32),
        ),
        in_specs=[pl.BlockSpec(memory_space=pltpu.HBM)] * 5,
        out_specs=(pl.BlockSpec(memory_space=pltpu.VMEM),) * 3,
        scratch_shapes=[
            vmem((T, DB), BF),
            vmem((T, DB), BF),
            vmem((2 * T, FB), BF),
            vmem((2, DB, FB), BF),
            vmem((FB, DB), BF),
            vmem((2, 2, 8, T, DB), BF),
            vmem((2, 2, 8, T, DB), BF),
            vmem((2, 2, 8, T, FB), BF),
            vmem((2, 2, 8, T, FB), BF),
            vmem((DB, TOK), BF),
            vmem((2, T, FB), F32),
            vmem((2, 8, T, FA), F32),
            vmem((2, 8, 2, T, FT), F32),
            vmem((2, 8, T, FA), BF),
            vmem((2, 8, T, FA), BF),
            vmem((2, 4, 2, T, FA), BF),
            vmem((2, 4, 2, T, FA), BF),
            vmem((2, 4, 2, 2, T, FT), BF),
            vmem((2, 4, 2, 2, T, FT), BF),
            vmem((2, T, FT), BF),
            vmem((2, T, FT), BF),
            vmem((8, 2, T, DB), F32),
            vmem((8, 2, T, DB), F32),
            vmem((8, 2, T, DB), BF),
            vmem((16, T, DB), BF),
            vmem((T, DB), F32),
        ]
        + [dma if s is None else dma(s) for s in sems],
        compiler_params=pltpu.CompilerParams(collective_id=0, has_side_effects=True, vmem_limit_bytes=48 * 2**20),
        cost_estimate=pl.CostEstimate(flops=8 * TOK * DB * FB, bytes_accessed=4 * 2**20, transcendentals=2 * 64 * FB),
        name="mlp_backward",
    )(*ins)


def solution(mesh):
    in_specs = (P("row", "col"), P("row", "col"), P("col", "row"), P("col", "row"), P("row", "col"))
    out_specs = (P("row", "col"), P("col", "row"), P("row", "col"))
    return jax.shard_map(on_device, mesh=mesh, in_specs=in_specs, out_specs=out_specs, check_vma=False)
```

time: 107 us -> 93.6 us (0.87)
  Pallas kernels: 101 us -> 90.1 us
  local copies, waits for them, and re-layouts: 4.82 us -> 2.64 us
    pallas_call x1, Pallas kernels: 101 us -> 90.1 us  [on_device(): pl.pallas_call(kernel, out_shape=(jax.ShapeDtypeStruct((T, DB), BF), jax....]
    unnamed x5 -> x3, local copies, waits for them, and re-layouts: 4.82 us -> 2.64 us
where the time goes in v3:
time: 93.6 us; the launch traced here: 93.4 us
  Pallas kernels  90.1 us (96%)
  local copies, waits for them, and re-layouts  2.64 us (3%)
    pallas_call x1, Pallas kernels, on_device(): pl.pallas_call(kernel, out_shape=(jax.ShapeDtypeStruct((T, DB), BF), jax....  90.1 us
    unnamed x3, local copies, waits for them, and re-layouts  2.64 us

profile of v3, /device:TPU:1, one launch (start us, length us, event | category | flops | bytes accessed | tf_op | source)
XLA Modules:
  0.0 93.4 jit_solution(1376236457361869657)
XLA Ops:
  0.6 90.1 %mlp_backward.1 = (bf16[32,384]{1,0:T(8,128)(2,1)S(1)}, f32[384,768]{1,0:T(8,128)S(1)}, f32[768,384]{1,0:T(8,128)S(1)}) custom-call(bf16[32,384]{1,0:T(8,128)(2,1)} %li.1, bf16[32,384]{1,0:T(8,128)(2,1)} %og.1, bf16[64,768]{1,0:T(8,128)(2,1)} %pre.1, bf16[384,768]{1,0:T(8,128)(2,1)} %w_in_hbm.1, bf16[768,384]{1,0:T(8,128)(2,1)} %w_out_hbm.1), custom_call_target="tpu_custom_call" | custom-call | flops 2415919104 | bytes 4194304 | tf_op jit(solution)/shard_map/mlp_backward/pallas_call | solution.py:337
  90.8 0.6 copy.11
  91.4 1.0 %copy.12 = f32[384,768]{1,0:T(8,128)} copy(f32[384,768]{1,0:T(8,128)S(1)} %get-tuple-element.7) | data formatting | bytes 2359296
  92.4 1.0 %copy.13 = f32[768,384]{1,0:T(8,128)} copy(f32[768,384]{1,0:T(8,128)S(1)} %get-tuple-element.8) | data formatting | bytes 2359296

commit v4 on v3

v4 whole, which is shorter than its diff:
```python
import math

import jax
import jax.numpy as jnp
from jax import lax
from jax.experimental import pallas as pl
from jax.experimental.pallas import tpu as pltpu
from jax.sharding import PartitionSpec as P

MESH = pl.DeviceIdType.MESH
BF, F32 = jnp.bfloat16, jnp.float32
TOK, DB, FB = 1024, 384, 768
T = 32
FT = 256
FA = 512


def gelu_parts(pre):
    cdf = 0.5 * (1.0 + lax.erf(pre * (1.0 / math.sqrt(2.0))))
    pdf = jnp.exp(-0.5 * pre * pre) * (1.0 / math.sqrt(2.0 * math.pi))
    return pre * cdf, cdf + pre * pdf


def dot(a, b, ca, cb):
    return lax.dot_general(a, b, (((ca,), (cb,)), ((), ())), preferred_element_type=F32)


def kernel(
    li, og, pre, w_in_hbm, w_out_hbm, ig_out, gi_out, go_out,
    li_v, og_v, pre_v, w_in, w_out, li_all, og_all, act_all, hid_all, li_t, slope, c_a, c_b, cz_send, cz_recv,
    ra_send, ra_recv, rb_send, rb_recv, bz_send, bz_recv, q_sib, q_in, q_send, q_recv, q_self,
    oz_ss, oz_rs, ox_ss, ox_rs, os_ss, os_rs, lz_ss, lz_rs, lx_ss, lx_rs, ls_ss, ls_rs,
    az_ss, az_rs, ay_ss, ay_rs, hy_ss, hy_rs, hz_ss, hz_rs, cz_ss, cz_rs, ra_ss, ra_rs, rb_ss, rb_rs, bz_ss, bz_rs,
    qs_ss, qs_rs, q_ss, q_rs, loc,
):
    row, col = lax.axis_index("row"), lax.axis_index("col")
    x, zh, k = row // 8, (row // 2) % 4, row % 2
    y, zl = col // 2, col % 2
    halves = (1 - k, k)
    my = 4 * x + zh

    def dev(x=x, zh=zh, k=k, y=y, zl=zl):
        return (x * 8 + zh * 2 + k, y * 2 + zl)

    sib, zpart = dev(k=1 - k), dev(zl=1 - zl)
    ynext = [dev(y=(y + 1) % 8), dev(y=(y + 7) % 8)]
    started = []

    def send(src, dst, ss, rs, to, cond=None):
        c = pltpu.make_async_remote_copy(src_ref=src, dst_ref=dst, send_sem=ss, recv_sem=rs, device_id=to, device_id_type=MESH)
        if cond is None:
            c.start()
        else:
            pl.when(cond)(c.start)
        started.append((cond, c))

    def arrive(dst, ss, rs):
        pltpu.make_async_remote_copy(src_ref=dst, dst_ref=dst, send_sem=ss, recv_sem=rs, device_id=sib, device_id_type=MESH).wait_recv()

    loads = [
        pltpu.make_async_copy(a, b, loc.at[i])
        for i, (a, b) in enumerate([(og, og_v), (pre, pre_v), (w_out_hbm, w_out), (w_in_hbm, w_in), (li, li_v)])
    ]
    for c in loads:
        c.start()

    barrier = pltpu.get_barrier_semaphore()
    greet = [dev(x=(x + a) % 4, zh=(zh + b) % 4) for a in range(4) for b in range(4) if (a, b) != (0, 0)]
    greet += [dev(x=(x + a) % 4, k=1 - k) for a in (1, 2, 3)] + ynext + [sib, zpart]
    for p in greet:
        pl.semaphore_signal(barrier, inc=1, device_id=p, device_id_type=MESH)
    loads[0].wait()
    pl.semaphore_wait(barrier, len(greet))

    def in_z(own, full, ss, rs):
        full[k, my] = own[...]
        for dz in (2, 1, 3):
            send(own, full.at[k, my], ss.at[dz - 1], rs.at[dz - 1], dev(zh=(zh + dz) % 4))

    def in_x(full, zss, zrs, ss, rs):
        for dz in (0, 1, 3, 2):
            ref = full.at[k, 4 * x + (zh + 4 - dz) % 4]
            if dz > 0:
                arrive(ref, zss.at[dz - 1], zrs.at[dz - 1])
            for dx in (2, 1, 3, 0):
                send(ref, ref, ss.at[dx, dz], rs.at[dx, dz], dev(x=(x + dx) % 4, k=1 - k))

    def in_core(full, xss, xrs, ss, rs):
        for dx in (0, 1, 3, 2):
            xs = (x + 4 - dx) % 4
            for dz in range(4):
                arrive(full.at[1 - k, 4 * xs + (zh + 4 - dz) % 4], xss.at[dx, dz], xrs.at[dx, dz])
            if dx > 0:
                ref = full.at[1 - k, pl.ds(4 * xs, 4)]
                send(ref, ref, ss.at[dx - 1], rs.at[dx - 1], sib)

    def in_done(full, ss, rs):
        for dx in (1, 3, 2):
            arrive(full.at[k, pl.ds(4 * ((x + 4 - dx) % 4), 4)], ss.at[dx - 1], rs.at[dx - 1])

    def swap(full, a, ss, rs):
        ref = full.at[halves[a], col]
        send(ref, ref, ss.at[a], rs.at[a], zpart)

    def ring(full, j, s, a, zss, zrs, ss, rs):
        zz = zl if j == 0 else 1 - zl
        if j == 1 and s == 0:
            arrive(full.at[halves[a], 2 * y + zz], zss.at[a], zrs.at[a])
        for d in range(2):
            hops = 4 if a == d else 3
            ref = full.at[halves[a], 2 * ((y + (8 - s if d == 0 else s)) % 8) + zz]
            if 0 < s <= hops:
                arrive(ref, ss.at[j, d, s - 1, a], rs.at[j, d, s - 1, a])
            if s < hops:
                send(ref, ref, ss.at[j, d, s, a], rs.at[j, d, s, a], ynext[d])

    in_z(og_v, og_all, oz_ss, oz_rs)
    loads[1].wait()
    for h in range(2):
        value, sl = gelu_parts(pre_v[pl.ds(h * T, T), :].astype(F32))
        act_all[h, col] = value.astype(BF)
        slope[h] = sl

    def act_step(j, s):
        for a in range(2):
            if j == 0 and s == 0:
                swap(act_all, a, az_ss, az_rs)
            ring(act_all, j, s, a, az_ss, az_rs, ay_ss, ay_rs)

    def hid_step(j, s, a):
        ring(hid_all, j, s, a, hz_ss, hz_rs, hy_ss, hy_rs)

    act_step(0, 0)
    act_step(0, 1)
    act_step(1, 0)
    in_x(og_all, oz_ss, oz_rs, ox_ss, ox_rs)
    act_step(1, 1)
    act_step(0, 2)
    loads[4].wait()
    in_core(og_all, ox_ss, ox_rs, os_ss, os_rs)

    def partial(a, n):
        return dot(og_all[halves[a]].reshape(16 * T, DB), w_out[pl.ds(n * FT, FT), :], 1, 1).reshape(8, 2, T, FT)

    def partials(a):
        h = halves[a]
        for n in (1, 2):
            c_a[h, :, :, :, pl.ds(n * FT - FT, FT)] = partial(a, n)
        for o in (4, 3, 5, 2, 6, 1, 7, 0):
            at = (y + o) % 8
            cz_send[h, at] = c_a[h, at, 1 - zl].astype(BF)
            send(cz_send.at[h, at], cz_recv.at[h, at], cz_ss.at[o, a], cz_rs.at[o, a], zpart)
        c_b[h] = partial(a, 0)
        rs_b(a, 0)

    def rs_b(a, s):
        h = halves[a]
        for d in range(2):
            hops = 3 if a == d else 4
            if s >= hops:
                continue
            to = hops - s
            total = c_b[h, (y + (to if d == 0 else 8 - to)) % 8]
            if s > 0:
                arrive(rb_recv.at[d, s - 1, a], rb_ss.at[d, s - 1, a], rb_rs.at[d, s - 1, a])
                total = total + rb_recv[d, s - 1, a].astype(F32)
            rb_send[d, s, a] = total.astype(BF)
            send(rb_send.at[d, s, a], rb_recv.at[d, s, a], rb_ss.at[d, s, a], rb_rs.at[d, s, a], ynext[d])

    def mine(a, o):
        h, at = halves[a], (y + o) % 8
        arrive(cz_recv.at[h, at], cz_ss.at[o, a], cz_rs.at[o, a])
        return c_a[h, at, zl] + cz_recv[h, at].astype(F32)

    def rs_a(a, s):
        for d in range(2):
            hops = 4 if a == d else 3
            if s >= hops:
                continue
            to = hops - s
            total = mine(a, to if d == 0 else 8 - to)
            if s > 0:
                arrive(ra_recv.at[d, s - 1, a], ra_ss.at[d, s - 1, a], ra_rs.at[d, s - 1, a])
                total = total + ra_recv[d, s - 1, a].astype(F32)
            ra_send[d, s, a] = total.astype(BF)
            send(ra_send.at[d, s, a], ra_recv.at[d, s, a], ra_ss.at[d, s, a], ra_rs.at[d, s, a], ynext[d])

    def last_b(a):
        h = halves[a]
        for d in range(2):
            s = 2 if a == d else 3
            arrive(rb_recv.at[d, s, a], rb_ss.at[d, s, a], rb_rs.at[d, s, a])
        bz_send[a] = (c_b[h, y, 1 - zl] + rb_recv[0, 2 if a == 0 else 3, a, 1 - zl].astype(F32) + rb_recv[1, 2 if a == 1 else 3, a, 1 - zl].astype(F32)).astype(BF)
        send(bz_send.at[a], bz_recv.at[a], bz_ss.at[a], bz_rs.at[a], zpart)

    def last_a(a):
        h = halves[a]
        total = mine(a, 0)
        for d in range(2):
            s = 3 if a == d else 2
            arrive(ra_recv.at[d, s, a], ra_ss.at[d, s, a], ra_rs.at[d, s, a])
            total = total + ra_recv[d, s, a].astype(F32)
        hid_all[h, col, :, pl.ds(FT, FA)] = (total * slope[h, :, pl.ds(FT, FA)]).astype(BF)
        total = c_b[h, y, zl] + rb_recv[0, 2 if a == 0 else 3, a, zl].astype(F32) + rb_recv[1, 2 if a == 1 else 3, a, zl].astype(F32)
        arrive(bz_recv.at[a], bz_ss.at[a], bz_rs.at[a])
        total = total + bz_recv[a].astype(F32)
        hid_all[h, col, :, pl.ds(0, FT)] = (total * slope[h, :, pl.ds(0, FT)]).astype(BF)

    loads[2].wait()
    partials(0)
    in_done(og_all, os_ss, os_rs)
    partials(1)
    act_step(1, 2)
    act_step(0, 3)
    in_z(li_v, li_all, lz_ss, lz_rs)
    rs_a(0, 0)
    rs_a(1, 0)
    rs_b(0, 1)
    rs_b(1, 1)
    rs_a(0, 1)
    rs_a(1, 1)
    act_step(1, 3)
    rs_b(0, 2)
    rs_b(1, 2)
    rs_a(0, 2)
    rs_a(1, 2)
    rs_b(0, 3)
    rs_b(1, 3)
    rs_a(0, 3)
    rs_a(1, 3)
    in_x(li_all, lz_ss, lz_rs, lx_ss, lx_rs)
    last_b(0)
    last_b(1)

    def q_part(a, offs):
        h = halves[a]
        at = [2 * ((y + o) % 8) for o in offs]
        rows = jnp.concatenate([hid_all[h, pl.ds(p, 2)].reshape(2 * T, FB) for p in at], axis=0)
        q = dot(rows, w_in[...], 1, 1)
        for i, (o, p) in enumerate(zip(offs, at, strict=True)):
            part = q[2 * i * T : 2 * (i + 1) * T].reshape(2, T, DB)
            if a == 0:
                q_sib[pl.ds(p, 2)] = part
                send(q_sib.at[pl.ds(p, 2)], q_in.at[pl.ds(p, 2)], qs_ss.at[o], qs_rs.at[o], sib)
                continue
            arrive(q_in.at[pl.ds(p, 2)], qs_ss.at[o], qs_rs.at[o])
            part = part + q_in[pl.ds(p, 2)]
            q_send[pl.ds(p, 2)] = part.astype(BF)
            for b in range(2):
                stays = p + b == my

                @pl.when(stays)
                def _():
                    q_self[...] = part[b]

                px, pz = (p + b) // 4, (p + b) % 4
                slot = (px + 4 - x) % 4 * 4 + (pz + 4 - zh) % 4
                send(q_send.at[p + b], q_recv.at[slot], q_ss.at[o, b], q_rs.at[slot], dev(x=px, zh=pz), jnp.logical_not(stays))

    def go_tile(n):
        cols = pl.ds(n * FT, FT)
        go_out[cols, :] = dot(act_all[:, :, :, cols].reshape(TOK, FT), og_all[...].reshape(TOK, DB), 0, 0)

    for a in range(2):
        last_a(a)
        swap(hid_all, a, hz_ss, hz_rs)
        hid_step(0, 0, a)
    act_step(0, 4)
    act_step(1, 4)
    go_tile(0)
    hid_step(1, 0, 0)
    hid_step(1, 0, 1)
    for j in range(2):
        hid_step(j, 1, 0)
        hid_step(j, 1, 1)
    go_tile(1)
    in_core(li_all, lx_ss, lx_rs, ls_ss, ls_rs)
    loads[3].wait()
    for j in range(2):
        hid_step(j, 2, 0)
        hid_step(j, 2, 1)
    q_part(0, (0, 1, 7, 2, 6))
    for j in range(2):
        hid_step(j, 3, 0)
        hid_step(j, 3, 1)
    q_part(1, (0, 1, 7, 2, 6))
    q_part(0, (3, 5))
    hid_step(0, 4, 0)
    hid_step(0, 4, 1)
    q_part(1, (3, 5))
    hid_step(1, 4, 0)
    q_part(0, (4,))
    hid_step(1, 4, 1)
    q_part(1, (4,))
    go_tile(2)
    in_done(li_all, ls_ss, ls_rs)
    li_t[...] = li_all[...].reshape(TOK, DB).T
    for n in range(3):
        cols = pl.ds(n * FT, FT)
        gi_out[:, cols] = dot(li_t[...], hid_all[:, :, :, cols].reshape(TOK, FT), 1, 0)
    total = q_self[...]
    for j in range(1, 16):
        arrive(q_recv.at[j], q_ss.at[0, 0], q_rs.at[j])
        total = total + q_recv[j].astype(F32)
    ig_out[...] = total.astype(BF)
    for cond, c in started:
        if cond is None:
            c.wait_send()
        else:
            pl.when(cond)(c.wait_send)


def on_device(layer_input, output_grad, preact, weight_in, weight_out):
    vmem, dma = pltpu.VMEM, pltpu.SemaphoreType.DMA
    ins = [pltpu.with_memory_space_constraint(a, pltpu.HBM) for a in (layer_input, output_grad, preact, weight_in, weight_out)]
    gather = [(3,), (3,), (4, 4), (4, 4), (3,), (3,)]
    sems = gather + gather
    sems += [s for s in [(2,), (2, 2, 4, 2), (2, 2, 4, 2), (2,), (8, 2), (2, 4, 2), (2, 4, 2), (2,), (8,)] for _ in range(2)]
    sems += [(8, 2), (16,), (5,)]
    return pl.pallas_call(
        kernel,
        out_shape=(
            jax.ShapeDtypeStruct((T, DB), BF),
            jax.ShapeDtypeStruct((DB, FB), F32),
            jax.ShapeDtypeStruct((FB, DB), F32),
        ),
        in_specs=[pl.BlockSpec(memory_space=pltpu.HBM)] * 5,
        out_specs=(pl.BlockSpec(memory_space=pltpu.VMEM),) * 3,
        scratch_shapes=[
            vmem((T, DB), BF),
            vmem((T, DB), BF),
            vmem((2 * T, FB), BF),
            vmem((DB, FB), BF),
            vmem((FB, DB), BF),
            vmem((2, 16, T, DB), BF),
            vmem((2, 16, T, DB), BF),
            vmem((2, 16, T, FB), BF),
            vmem((2, 16, T, FB), BF),
            vmem((DB, TOK), BF),
            vmem((2, T, FB), F32),
            vmem((2, 8, 2, T, FA), F32),
            vmem((2, 8, 2, T, FT), F32),
            vmem((2, 8, T, FA), BF),
            vmem((2, 8, T, FA), BF),
            vmem((2, 4, 2, T, FA), BF),
            vmem((2, 4, 2, T, FA), BF),
            vmem((2, 4, 2, 2, T, FT), BF),
            vmem((2, 4, 2, 2, T, FT), BF),
            vmem((2, T, FT), BF),
            vmem((2, T, FT), BF),
            vmem((16, T, DB), F32),
            vmem((16, T, DB), F32),
            vmem((16, T, DB), BF),
            vmem((16, T, DB), BF),
            vmem((T, DB), F32),
        ]
        + [dma(s) for s in sems],
        compiler_params=pltpu.CompilerParams(collective_id=0, has_side_effects=True, vmem_limit_bytes=48 * 2**20),
        cost_estimate=pl.CostEstimate(flops=8 * TOK * DB * FB, bytes_accessed=4 * 2**20, transcendentals=2 * 64 * FB),
        name="mlp_backward",
    )(*ins)


def solution(mesh):
    in_specs = (P("row", "col"), P("row", "col"), P("col", "row"), P("col", "row"), P("row", "col"))
    out_specs = (P("row", "col"), P("col", "row"), P("row", "col"))
    return jax.shard_map(on_device, mesh=mesh, in_specs=in_specs, out_specs=out_specs, check_vma=False)
```

time: 93.6 us -> 84.3 us (0.901)
  the two profiles are of different devices: /device:TPU:1 before, /device:TPU:24 now
where the time goes in v4:
time: 84.3 us; the launch traced here: 84.2 us
  Pallas kernels  80.9 us (96%)
  local copies, waits for them, and re-layouts  2.64 us (3%)
    pallas_call x1, Pallas kernels, on_device(): pl.pallas_call(kernel, out_shape=(jax.ShapeDtypeStruct((T, DB), BF), jax....  80.9 us
    unnamed x3, local copies, waits for them, and re-layouts  2.64 us

profile of v4, /device:TPU:24, one launch (start us, length us, event | category | flops | bytes accessed | tf_op | source)
XLA Modules:
  0.0 84.2 jit_solution(4190068843143775495)
XLA Ops:
  0.6 80.9 %mlp_backward.1 = (bf16[32,384]{1,0:T(8,128)(2,1)S(1)}, f32[384,768]{1,0:T(8,128)S(1)}, f32[768,384]{1,0:T(8,128)S(1)}) custom-call(bf16[32,384]{1,0:T(8,128)(2,1)} %li.1, bf16[32,384]{1,0:T(8,128)(2,1)} %og.1, bf16[64,768]{1,0:T(8,128)(2,1)} %pre.1, bf16[384,768]{1,0:T(8,128)(2,1)} %w_in_hbm.1, bf16[768,384]{1,0:T(8,128)(2,1)} %w_out_hbm.1), custom_call_target="tpu_custom_call" | custom-call | flops 2415919104 | bytes 4194304 | tf_op jit(solution)/shard_map/mlp_backward/pallas_call | solution.py:320
  81.5 0.6 copy.11
  82.1 1.0 %copy.12 = f32[384,768]{1,0:T(8,128)} copy(f32[384,768]{1,0:T(8,128)S(1)} %get-tuple-element.7) | data formatting | bytes 2359296
  83.1 1.0 %copy.13 = f32[768,384]{1,0:T(8,128)} copy(f32[768,384]{1,0:T(8,128)S(1)} %get-tuple-element.8) | data formatting | bytes 2359296

commit v5 on v4

--- a/solution.py
+++ b/solution.py
@@ -54,6 +54,14 @@
             pl.when(cond)(c.start)
         started.append((cond, c))
 
+    def drain(n):
+        for cond, c in started[:n]:
+            if cond is None:
+                c.wait_send()
+            else:
+                pl.when(cond)(c.wait_send)
+        del started[:n]
+
     def arrive(dst, ss, rs):
         pltpu.make_async_remote_copy(src_ref=dst, dst_ref=dst, send_sem=ss, recv_sem=rs, device_id=sib, device_id_type=MESH).wait_recv()
 
@@ -142,14 +150,19 @@
     def partial(a, n):
         return dot(og_all[halves[a]].reshape(16 * T, DB), w_out[pl.ds(n * FT, FT), :], 1, 1).reshape(8, 2, T, FT)
 
-    def partials(a):
-        h = halves[a]
-        for n in (1, 2):
-            c_a[h, :, :, :, pl.ds(n * FT - FT, FT)] = partial(a, n)
-        for o in (4, 3, 5, 2, 6, 1, 7, 0):
+    def to_partner(a, s):
+        h = halves[a]
+        for o in (((4, 5), (3, 6), (2, 7), (1, 0)), ((4, 3), (5, 2), (6, 1), (7, 0)))[a][s]:
             at = (y + o) % 8
             cz_send[h, at] = c_a[h, at, 1 - zl].astype(BF)
             send(cz_send.at[h, at], cz_recv.at[h, at], cz_ss.at[o, a], cz_rs.at[o, a], zpart)
+
+    def partials(a):
+        h = halves[a]
+        for n in (1, 2):
+            c_a[h, :, :, :, pl.ds(n * FT - FT, FT)] = partial(a, n)
+        to_partner(a, 0)
+        to_partner(a, 1)
         c_b[h] = partial(a, 0)
         rs_b(a, 0)
 
@@ -184,6 +197,8 @@
                 total = total + ra_recv[d, s - 1, a].astype(F32)
             ra_send[d, s, a] = total.astype(BF)
             send(ra_send.at[d, s, a], ra_recv.at[d, s, a], ra_ss.at[d, s, a], ra_rs.at[d, s, a], ynext[d])
+        if s < 2:
+            to_partner(a, s + 2)
 
     def last_b(a):
         h = halves[a]
@@ -208,10 +223,10 @@
 
     loads[2].wait()
     partials(0)
+    act_step(1, 2)
+    act_step(0, 3)
     in_done(og_all, os_ss, os_rs)
     partials(1)
-    act_step(1, 2)
-    act_step(0, 3)
     in_z(li_v, li_all, lz_ss, lz_rs)
     rs_a(0, 0)
     rs_a(1, 0)
@@ -261,6 +276,7 @@
         cols = pl.ds(n * FT, FT)
         go_out[cols, :] = dot(act_all[:, :, :, cols].reshape(TOK, FT), og_all[...].reshape(TOK, DB), 0, 0)
 
+    old = len(started)
     for a in range(2):
         last_a(a)
         swap(hid_all, a, hz_ss, hz_rs)
@@ -274,6 +290,7 @@
         hid_step(j, 1, 0)
         hid_step(j, 1, 1)
     go_tile(1)
+    drain(old)
     in_core(li_all, lx_ss, lx_rs, ls_ss, ls_rs)
     loads[3].wait()
     for j in range(2):
@@ -289,6 +306,7 @@
     hid_step(0, 4, 1)
     q_part(1, (3, 5))
     hid_step(1, 4, 0)
+    old = len(started)
     q_part(0, (4,))
     hid_step(1, 4, 1)
     q_part(1, (4,))
@@ -298,16 +316,13 @@
     for n in range(3):
         cols = pl.ds(n * FT, FT)
         gi_out[:, cols] = dot(li_t[...], hid_all[:, :, :, cols].reshape(TOK, FT), 1, 0)
+    drain(old)
     total = q_self[...]
     for j in range(1, 16):
         arrive(q_recv.at[j], q_ss.at[0, 0], q_rs.at[j])
         total = total + q_recv[j].astype(F32)
     ig_out[...] = total.astype(BF)
-    for cond, c in started:
-        if cond is None:
-            c.wait_send()
-        else:
-            pl.when(cond)(c.wait_send)
+    drain(len(started))
 
 
 def on_device(layer_input, output_grad, preact, weight_in, weight_out):

time: 84.3 us -> 81.1 us (0.962)
  Pallas kernels: 80.9 us -> 77.7 us
    pallas_call x1, Pallas kernels: 80.9 us -> 77.7 us  [on_device(): pl.pallas_call(kernel, out_shape=(jax.ShapeDtypeStruct((T, DB), BF), jax....]
where the time goes in v5:
time: 81.1 us; the launch traced here: 80.9 us
  Pallas kernels  77.7 us (96%)
  local copies, waits for them, and re-layouts  2.64 us (3%)
    pallas_call x1, Pallas kernels, on_device(): pl.pallas_call(kernel, out_shape=(jax.ShapeDtypeStruct((T, DB), BF), jax....  77.7 us
    unnamed x3, local copies, waits for them, and re-layouts  2.64 us

profile of v5, /device:TPU:24, one launch (start us, length us, event | category | flops | bytes accessed | tf_op | source)
XLA Modules:
  0.0 80.9 jit_solution(9882466953498032171)
XLA Ops:
  0.6 77.7 %mlp_backward.1 = (bf16[32,384]{1,0:T(8,128)(2,1)S(1)}, f32[384,768]{1,0:T(8,128)S(1)}, f32[768,384]{1,0:T(8,128)S(1)}) custom-call(bf16[32,384]{1,0:T(8,128)(2,1)} %li.1, bf16[32,384]{1,0:T(8,128)(2,1)} %og.1, bf16[64,768]{1,0:T(8,128)(2,1)} %pre.1, bf16[384,768]{1,0:T(8,128)(2,1)} %w_in_hbm.1, bf16[768,384]{1,0:T(8,128)(2,1)} %w_out_hbm.1), custom_call_target="tpu_custom_call" | custom-call | flops 2415919104 | bytes 4194304 | tf_op jit(solution)/shard_map/mlp_backward/pallas_call | solution.py:335
  78.3 0.6 copy.11
  78.9 1.0 %copy.12 = f32[384,768]{1,0:T(8,128)} copy(f32[384,768]{1,0:T(8,128)S(1)} %get-tuple-element.7) | data formatting | bytes 2359296
  79.9 1.0 %copy.13 = f32[768,384]{1,0:T(8,128)} copy(f32[768,384]{1,0:T(8,128)S(1)} %get-tuple-element.8) | data formatting | bytes 2359296

commit v6 on v5

--- a/solution.py
+++ b/solution.py
@@ -30,7 +30,7 @@
     li_v, og_v, pre_v, w_in, w_out, li_all, og_all, act_all, hid_all, li_t, slope, c_a, c_b, cz_send, cz_recv,
     ra_send, ra_recv, rb_send, rb_recv, bz_send, bz_recv, q_sib, q_in, q_send, q_recv, q_self,
     oz_ss, oz_rs, ox_ss, ox_rs, os_ss, os_rs, lz_ss, lz_rs, lx_ss, lx_rs, ls_ss, ls_rs,
-    az_ss, az_rs, ay_ss, ay_rs, hy_ss, hy_rs, hz_ss, hz_rs, cz_ss, cz_rs, ra_ss, ra_rs, rb_ss, rb_rs, bz_ss, bz_rs,
+    az_ss, az_rs, ay_ss, ay_rs, hy_ss, hy_rs, hz_ss, hz_rs, hp_ss, hp_rs, cz_ss, cz_rs, ra_ss, ra_rs, rb_ss, rb_rs, bz_ss, bz_rs,
     qs_ss, qs_rs, q_ss, q_rs, loc,
 ):
     row, col = lax.axis_index("row"), lax.axis_index("col")
@@ -110,12 +110,12 @@
         ref = full.at[halves[a], col]
         send(ref, ref, ss.at[a], rs.at[a], zpart)
 
-    def ring(full, j, s, a, zss, zrs, ss, rs):
+    def ring(full, j, s, a, zss, zrs, ss, rs, reach=4):
         zz = zl if j == 0 else 1 - zl
         if j == 1 and s == 0:
             arrive(full.at[halves[a], 2 * y + zz], zss.at[a], zrs.at[a])
         for d in range(2):
-            hops = 4 if a == d else 3
+            hops = min(4 if a == d else 3, reach)
             ref = full.at[halves[a], 2 * ((y + (8 - s if d == 0 else s)) % 8) + zz]
             if 0 < s <= hops:
                 arrive(ref, ss.at[j, d, s - 1, a], rs.at[j, d, s - 1, a])
@@ -136,7 +136,16 @@
             ring(act_all, j, s, a, az_ss, az_rs, ay_ss, ay_rs)
 
     def hid_step(j, s, a):
-        ring(hid_all, j, s, a, hz_ss, hz_rs, hy_ss, hy_rs)
+        ring(hid_all, j, s, a, hz_ss, hz_rs, hy_ss, hy_rs, 4 if j == 0 else 2)
+        if j == 0 and s >= 3:
+            for o in (5, 3) if s == 3 else (4,):
+                ref = hid_all.at[halves[a], 2 * ((y + o) % 8) + zl]
+                send(ref, ref, hp_ss.at[o - 3, a], hp_rs.at[o - 3, a], zpart)
+
+    def passed(a, offs):
+        for o in offs:
+            ref = hid_all.at[halves[a], 2 * ((y + o) % 8) + 1 - zl]
+            arrive(ref, hp_ss.at[o - 3, a], hp_rs.at[o - 3, a])
 
     act_step(0, 0)
     act_step(0, 1)
@@ -297,18 +306,19 @@
         hid_step(j, 2, 0)
         hid_step(j, 2, 1)
     q_part(0, (0, 1, 7, 2, 6))
-    for j in range(2):
-        hid_step(j, 3, 0)
-        hid_step(j, 3, 1)
+    hid_step(0, 3, 0)
+    hid_step(0, 3, 1)
     q_part(1, (0, 1, 7, 2, 6))
-    q_part(0, (3, 5))
     hid_step(0, 4, 0)
     hid_step(0, 4, 1)
+    passed(0, (3, 5))
+    q_part(0, (3, 5))
+    passed(1, (3, 5))
     q_part(1, (3, 5))
-    hid_step(1, 4, 0)
     old = len(started)
+    passed(0, (4,))
     q_part(0, (4,))
-    hid_step(1, 4, 1)
+    passed(1, (4,))
     q_part(1, (4,))
     go_tile(2)
     in_done(li_all, ls_ss, ls_rs)
@@ -330,7 +340,7 @@
     ins = [pltpu.with_memory_space_constraint(a, pltpu.HBM) for a in (layer_input, output_grad, preact, weight_in, weight_out)]
     gather = [(3,), (3,), (4, 4), (4, 4), (3,), (3,)]
     sems = gather + gather
-    sems += [s for s in [(2,), (2, 2, 4, 2), (2, 2, 4, 2), (2,), (8, 2), (2, 4, 2), (2, 4, 2), (2,), (8,)] for _ in range(2)]
+    sems += [s for s in [(2,), (2, 2, 4, 2), (2, 2, 4, 2), (2,), (3, 2), (8, 2), (2, 4, 2), (2, 4, 2), (2,), (8,)] for _ in range(2)]
     sems += [(8, 2), (16,), (5,)]
     return pl.pallas_call(
         kernel,

time: 81.1 us -> 86.3 us (1.064)
  the two profiles are of different devices: /device:TPU:24 before, /device:TPU:4 now
where the time goes in v6:
time: 86.3 us; the launch traced here: 86.2 us
  Pallas kernels  82.9 us (96%)
  local copies, waits for them, and re-layouts  2.64 us (3%)
    pallas_call x1, Pallas kernels, on_device(): pl.pallas_call(kernel, out_shape=(jax.ShapeDtypeStruct((T, DB), BF), jax....  82.9 us
    unnamed x3, local copies, waits for them, and re-layouts  2.64 us

profile of v6, /device:TPU:4, one launch (start us, length us, event | category | flops | bytes accessed | tf_op | source)
XLA Modules:
  0.0 86.2 jit_solution(11943618555539618918)
XLA Ops:
  0.6 82.9 %mlp_backward.1 = (bf16[32,384]{1,0:T(8,128)(2,1)S(1)}, f32[384,768]{1,0:T(8,128)S(1)}, f32[768,384]{1,0:T(8,128)S(1)}) custom-call(bf16[32,384]{1,0:T(8,128)(2,1)} %li.1, bf16[32,384]{1,0:T(8,128)(2,1)} %og.1, bf16[64,768]{1,0:T(8,128)(2,1)} %pre.1, bf16[384,768]{1,0:T(8,128)(2,1)} %w_in_hbm.1, bf16[768,384]{1,0:T(8,128)(2,1)} %w_out_hbm.1), custom_call_target="tpu_custom_call" | custom-call | flops 2415919104 | bytes 4194304 | tf_op jit(solution)/shard_map/mlp_backward/pallas_call | solution.py:345
  83.5 0.6 copy.11
  84.1 1.0 %copy.12 = f32[384,768]{1,0:T(8,128)} copy(f32[384,768]{1,0:T(8,128)S(1)} %get-tuple-element.7) | data formatting | bytes 2359296
  85.2 1.0 %copy.13 = f32[768,384]{1,0:T(8,128)} copy(f32[768,384]{1,0:T(8,128)S(1)} %get-tuple-element.8) | data formatting | bytes 2359296
